TPU v7x, 256 devices: a whole 4x4x8 slice. The times are simulated.
256 devices in a mesh: row: 16 (over z_hi, x), col: 16 (over z_lo, y, core).
Axes of the slice: x: 4, y: 4, z: 8 (z_hi: 4, z_lo: 2; z = z_hi * 2 + z_lo), core: 2. Of those that a mesh axis runs over, the one named last changes fastest.
Arguments:
- features: bfloat16 [196608, 256], P(('row', 'col')), may hold values from -6 to 6
- node_order: int32 [256, 768], P(('row', 'col')), may hold values from 0 to 767, each once within a row
- block_rows: int32 [16, 16, 192], P('row', 'col'), may hold values from 0 to 95
- block_cols: int32 [16, 16, 192], P('row', 'col'), may hold values from 0 to 95
- block_counts: int32 [16, 16], P('row', 'col'), may hold values from 32 to 192, as said below
- adjacency: bfloat16 [16, 16, 192, 128, 128], P('row', 'col'), may hold values from -0.125 to 0.125
- weight_one: bfloat16 [256, 256], replicated, may hold values from -0.375 to 0.375
- weight_two: bfloat16 [256, 256], replicated, may hold values from -0.375 to 0.375
Outputs:
- embeddings: bfloat16 [196608, 256], P(('row', 'col'))
Inputs may be any that keep to these rules, and one draw needn't show every extreme that they name: `block_counts`: every tile uses between 32 and 192 slots; some tile uses all 192. `block_rows`: coordinates may repeat within a tile.
All inputs are finite; a program needn't handle non-finite values.
Results may differ from a plain program's by a relative error of at most 0.028.
Values may be sent and summed in bfloat16 or wider, within the bound.
A program may use at most 128 MiB of HBM per device.

v0:
```python
import jax
import jax.numpy as jnp
from jax import lax
from jax.sharding import PartitionSpec as P


def block_product(
    panel_rows, tile_values, source_ids, target_ids, live_count, out_blocks, transposed
):
    block_size = tile_values.shape[-1]
    slot_count = tile_values.shape[0]
    stride = min(64, slot_count)
    feature_width = panel_rows.shape[1]
    tile_set = panel_rows.reshape(panel_rows.shape[0] // block_size, block_size, feature_width)
    target_grid = jnp.arange(out_blocks, dtype=jnp.int32)
    pattern = "bji,bjk->bik" if transposed else "bij,bjk->bik"

    def accumulate(round_index, carried):
        offset = round_index * stride
        blocks_now = lax.dynamic_slice_in_dim(tile_values, offset, stride, 0)
        source_now = lax.dynamic_slice_in_dim(source_ids, offset, stride, 0)
        target_now = lax.dynamic_slice_in_dim(target_ids, offset, stride, 0)
        chosen = jnp.take(tile_set, source_now, axis=0)
        product = jnp.einsum(pattern, blocks_now, chosen, preferred_element_type=jnp.float32)
        active = offset + jnp.arange(stride, dtype=jnp.int32) < live_count
        selector = jnp.where(
            (target_now[None, :] == target_grid[:, None]) & active[None, :], 1.0, 0.0
        ).astype(jnp.float32)
        return carried + jnp.einsum("gb,bik->gik", selector, product)

    rounds = slot_count // stride
    summed = lax.fori_loop(
        0, rounds, accumulate, jnp.zeros((out_blocks, block_size, feature_width), jnp.float32)
    )
    return summed.reshape(out_blocks * block_size, feature_width)


def on_device(
    features, node_order, block_rows, block_cols, block_counts, adjacency, weight_one, weight_two
):
    initial = jnp.take(features, node_order[0], axis=0)
    tiles_here = adjacency[0, 0]
    rows_here = block_rows[0, 0]
    cols_here = block_cols[0, 0]
    live_count = block_counts[0, 0]
    block_size = tiles_here.shape[-1]
    row_group = initial.shape[0] * lax.axis_size("col")
    col_group = initial.shape[0] * lax.axis_size("row")
    row_panel = lax.all_gather(initial, "col", axis=0, tiled=True)
    partial_one = block_product(
        row_panel, tiles_here, rows_here, cols_here, live_count, col_group // block_size, True
    )
    summed = lax.psum_scatter(
        partial_one.astype(jnp.bfloat16), "row", scatter_dimension=0, tiled=True
    )
    hidden = jax.nn.relu(jnp.dot(summed, weight_one, preferred_element_type=jnp.float32)).astype(
        jnp.bfloat16
    )
    col_panel = lax.all_gather(hidden, "row", axis=0, tiled=True)
    partial_two = block_product(
        col_panel, tiles_here, cols_here, rows_here, live_count, row_group // block_size, False
    )
    second = lax.psum_scatter(
        partial_two.astype(jnp.bfloat16), "col", scatter_dimension=0, tiled=True
    )
    return jax.nn.relu(jnp.dot(second, weight_two, preferred_element_type=jnp.float32)).astype(
        jnp.bfloat16
    )


def solution(mesh):
    in_specs = (
        P(("row", "col"), None),
        P(("row", "col"), None),
        P("row", "col", None),
        P("row", "col", None),
        P("row", "col"),
        P("row", "col", None, None, None),
        P(),
        P(),
    )
    out_specs = P(("row", "col"), None)
    return jax.shard_map(
        on_device, mesh=mesh, in_specs=in_specs, out_specs=out_specs, check_vma=False
    )
```

profile of v0, /device:TPU:1, one launch (start us, length us, event | category | flops | bytes accessed | tf_op | source)
XLA Modules:
  0.0 531.1 jit_solution(442469603547994244)
XLA Ops:
  6.5 0.7 fusion.48
  7.3 0.7 reduce
  8.0 2.7 gather_fusion.2
  10.7 0.9 broadcast_select_fusion
  11.6 0.0 all-gather.3.cloned.1.call-update
  11.6 0.0 reduce-scatter.3.cloned.1.call-start
  11.7 49.3 %all-gather.3.cloned.1.call-done = bf16[12288,256]{1,0:T(8,128)(2,1)} async-done(((bf16[768,256]{1,0:T(8,128)(2,1)}), bf16[12288,256]{1,0:T(8,128)(2,1)}) %all-gather.3.cloned.1.call-update) | async-done | bytes 6291472 | tf_op jit(solution)/shard_map/all_gather | solution.py:49
  61.0 78.2 %while.28 = (s32[]{:T(128)}, f32[96,128,256]{2,0,1:T(8,128)}, s32[192]{0:T(256)S(1)}, s32[]{:T(128)}, bf16[192,128,128]{2,1,0:T(8,128)(2,1)}, /*index=5*/s32[192...) while((s32[]{:T(128)}, f32[96,128,256]{2,0,1:T(8,128)}, ...), condition=%wide.region_1.3_spmd.clone, body=%wide.region_0.0_spmd.clone.sunk | while | flops 947932672 | bytes 48240824 | solution.py:32
  61.0 0.7 compare_and_fusion.5
  61.7 5.6 %gather_fusion = bf16[64,128,256]{2,1,0:T(8,128)(2,1)} fusion(bf16[96,128,256]{2,1,0:T(8,128)(2,1)} %get-tuple-element.498, s32[1024]{0:T(1024)S(1)} %pad_clamp_fusion.5), kind=kCustom, calls=%fused_computation.clone.clone.1 | custom fusion | bytes 8388864 | tf_op jit(solution)/shard_map/while/body/eval_jaxpr/jit(_take)/gather | solution.py:23
  67.3 6.2 %fusion.67 = bf16[64,128,256]{2,1,0:T(8,128)(2,1)} fusion(bf16[64,128,256]{2,1,0:T(8,128)(2,1)} %gather_fusion, pred[64]{0:T(512)(128)(4,1)S(1)} %get-tuple-element.458, bf16[192,128,128]{2,1,0:T(8,128)(2,1)} %get-tuple-element.496, s32[]{:T(128)S(6)} %select_n.104), kind=kOutput, calls=%fused_computation.8.clone.1 | convolution fusion | flops 538968064 | bytes 10485828 | tf_op jit(solution)/shard_map/while/body/eval_jaxpr/bji,bjk->bik/dot_general | solution.py:24
  73.5 0.1 dynamic_slice.61
  73.6 11.0 %select_add_fusion.4 = f32[96,128,256]{2,0,1:T(8,128)} fusion(f32[96,128,256]{2,0,1:T(8,128)} %get-tuple-element.482, pred[]{:T(512)S(6)} %compare.6, bf16[64,128,256]{2,1,0:T(8,128)(2,1)} %fusion.67, s32[64]{0:T(128)S(1)} %dynamic_slice.61, pred[64]{0:T(512)(128)(4,1)S(1)} %get-tuple-element.459), kind=kOutput, calls=%fused_computation.5.clone.1 | convolution fusion | flops 408963072 | bytes 29360448 | tf_op jit(solution)/shard_map/while/body/eval_jaxpr/gb,bik->gik/dot_general | solution.py:29
  84.6 0.7 compare_and_fusion.5
  85.3 5.6 %gather_fusion = bf16[64,128,256]{2,1,0:T(8,128)(2,1)} fusion(bf16[96,128,256]{2,1,0:T(8,128)(2,1)} %get-tuple-element.498, s32[1024]{0:T(1024)S(1)} %pad_clamp_fusion.5), kind=kCustom, calls=%fused_computation.clone.clone.1 | custom fusion | bytes 8388864 | tf_op jit(solution)/shard_map/while/body/eval_jaxpr/jit(_take)/gather | solution.py:23
  90.9 6.2 %fusion.67 = bf16[64,128,256]{2,1,0:T(8,128)(2,1)} fusion(bf16[64,128,256]{2,1,0:T(8,128)(2,1)} %gather_fusion, pred[64]{0:T(512)(128)(4,1)S(1)} %get-tuple-element.458, bf16[192,128,128]{2,1,0:T(8,128)(2,1)} %get-tuple-element.496, s32[]{:T(128)S(6)} %select_n.104), kind=kOutput, calls=%fused_computation.8.clone.1 | convolution fusion | flops 538968064 | bytes 10485828 | tf_op jit(solution)/shard_map/while/body/eval_jaxpr/bji,bjk->bik/dot_general | solution.py:24
  97.2 0.1 dynamic_slice.61
  97.2 14.6 %select_add_fusion.4 = f32[96,128,256]{2,0,1:T(8,128)} fusion(f32[96,128,256]{2,0,1:T(8,128)} %get-tuple-element.482, pred[]{:T(512)S(6)} %compare.6, bf16[64,128,256]{2,1,0:T(8,128)(2,1)} %fusion.67, s32[64]{0:T(128)S(1)} %dynamic_slice.61, pred[64]{0:T(512)(128)(4,1)S(1)} %get-tuple-element.459), kind=kOutput, calls=%fused_computation.5.clone.1 | convolution fusion | flops 408963072 | bytes 29360448 | tf_op jit(solution)/shard_map/while/body/eval_jaxpr/gb,bik->gik/dot_general | solution.py:29
  111.9 0.7 compare_and_fusion.5
  112.6 5.6 %gather_fusion = bf16[64,128,256]{2,1,0:T(8,128)(2,1)} fusion(bf16[96,128,256]{2,1,0:T(8,128)(2,1)} %get-tuple-element.498, s32[1024]{0:T(1024)S(1)} %pad_clamp_fusion.5), kind=kCustom, calls=%fused_computation.clone.clone.1 | custom fusion | bytes 8388864 | tf_op jit(solution)/shard_map/while/body/eval_jaxpr/jit(_take)/gather | solution.py:23
  118.2 6.2 %fusion.67 = bf16[64,128,256]{2,1,0:T(8,128)(2,1)} fusion(bf16[64,128,256]{2,1,0:T(8,128)(2,1)} %gather_fusion, pred[64]{0:T(512)(128)(4,1)S(1)} %get-tuple-element.458, bf16[192,128,128]{2,1,0:T(8,128)(2,1)} %get-tuple-element.496, s32[]{:T(128)S(6)} %select_n.104), kind=kOutput, calls=%fused_computation.8.clone.1 | convolution fusion | flops 538968064 | bytes 10485828 | tf_op jit(solution)/shard_map/while/body/eval_jaxpr/bji,bjk->bik/dot_general | solution.py:24
  124.4 0.1 dynamic_slice.61
  124.5 14.6 %select_add_fusion.4 = f32[96,128,256]{2,0,1:T(8,128)} fusion(f32[96,128,256]{2,0,1:T(8,128)} %get-tuple-element.482, pred[]{:T(512)S(6)} %compare.6, bf16[64,128,256]{2,1,0:T(8,128)(2,1)} %fusion.67, s32[64]{0:T(128)S(1)} %dynamic_slice.61, pred[64]{0:T(512)(128)(4,1)S(1)} %get-tuple-element.459), kind=kOutput, calls=%fused_computation.5.clone.1 | convolution fusion | flops 408963072 | bytes 29360448 | tf_op jit(solution)/shard_map/while/body/eval_jaxpr/gb,bik->gik/dot_general | solution.py:29
  139.2 13.8 %copy.24 = bf16[96,128,256]{2,1,0:T(8,128)(2,1)} copy(f32[96,128,256]{2,0,1:T(8,128)} %get-tuple-element.284) | data formatting | bytes 18874368 | tf_op jit(solution)/shard_map/while | solution.py:32
  153.0 0.0 all-gather.5.cloned.1.call-start
  153.1 109.4 %reduce-scatter.3.cloned.1.call-done = bf16[768,256]{1,0:T(8,128)(2,1)} async-done(((bf16[12288,256]{1,0:T(8,128)(2,1)}), bf16[768,256]{1,0:T(8,128)(2,1)}) %reduce-scatter.3.cloned.1.call-update) | async-done | bytes 393232 | tf_op jit(solution)/shard_map/reduce_scatter | solution.py:53
  262.5 2.0 fusion.46
  264.6 0.0 reduce-scatter.5.cloned.1.call-start
  264.6 91.3 %all-gather.5.cloned.1.call-done = bf16[12288,256]{1,0:T(8,128)(2,1)} async-done(((bf16[768,256]{1,0:T(8,128)(2,1)}), bf16[12288,256]{1,0:T(8,128)(2,1)}) %all-gather.5.cloned.1.call-update) | async-done | bytes 6291472 | tf_op jit(solution)/shard_map/all_gather | solution.py:59
  355.9 78.1 %while.29 = (s32[]{:T(128)}, f32[96,128,256]{2,0,1:T(8,128)}, s32[192]{0:T(256)S(1)}, s32[]{:T(128)}, bf16[192,128,128]{2,1,0:T(8,128)(2,1)}, /*index=5*/s32[192...) while((s32[]{:T(128)}, f32[96,128,256]{2,0,1:T(8,128)}, ...), condition=%wide.region_4.6_spmd.clone, body=%wide.region_3.5_spmd.clone.sunk | while | flops 947932672 | bytes 48240824 | solution.py:32
  355.9 0.7 compare_and_fusion.6
  356.7 5.6 %gather_fusion.1 = bf16[64,128,256]{2,1,0:T(8,128)(2,1)} fusion(bf16[96,128,256]{2,1,0:T(8,128)(2,1)} %get-tuple-element.531, s32[1024]{0:T(1024)S(1)} %pad_clamp_fusion.6), kind=kCustom, calls=%fused_computation.1.clone.clone.1 | custom fusion | bytes 8388864 | tf_op jit(solution)/shard_map/while/body/eval_jaxpr/jit(_take)/gather | solution.py:23
  362.3 6.2 %fusion.72 = bf16[64,128,256]{2,1,0:T(8,128)(2,1)} fusion(bf16[64,128,256]{2,1,0:T(8,128)(2,1)} %gather_fusion.1, pred[64]{0:T(512)(128)(4,1)S(1)} %get-tuple-element.468, bf16[192,128,128]{2,1,0:T(8,128)(2,1)} %get-tuple-element.529, s32[]{:T(128)S(6)} %select_n.107), kind=kOutput, calls=%fused_computation.32.clone.1 | convolution fusion | flops 538968064 | bytes 10485828 | tf_op jit(solution)/shard_map/while/body/eval_jaxpr/bij,bjk->bik/dot_general | solution.py:24
  368.5 0.1 dynamic_slice.63
  368.5 11.0 %select_add_fusion.5 = f32[96,128,256]{2,0,1:T(8,128)} fusion(f32[96,128,256]{2,0,1:T(8,128)} %get-tuple-element.515, pred[]{:T(512)S(6)} %compare.7, bf16[64,128,256]{2,1,0:T(8,128)(2,1)} %fusion.72, s32[64]{0:T(128)S(1)} %dynamic_slice.63, pred[64]{0:T(512)(128)(4,1)S(1)} %get-tuple-element.469), kind=kOutput, calls=%fused_computation.29.clone.1 | convolution fusion | flops 408963072 | bytes 29360448 | tf_op jit(solution)/shard_map/while/body/eval_jaxpr/gb,bik->gik/dot_general | solution.py:29
  379.5 0.7 compare_and_fusion.6
  380.2 5.6 %gather_fusion.1 = bf16[64,128,256]{2,1,0:T(8,128)(2,1)} fusion(bf16[96,128,256]{2,1,0:T(8,128)(2,1)} %get-tuple-element.531, s32[1024]{0:T(1024)S(1)} %pad_clamp_fusion.6), kind=kCustom, calls=%fused_computation.1.clone.clone.1 | custom fusion | bytes 8388864 | tf_op jit(solution)/shard_map/while/body/eval_jaxpr/jit(_take)/gather | solution.py:23
  385.9 6.2 %fusion.72 = bf16[64,128,256]{2,1,0:T(8,128)(2,1)} fusion(bf16[64,128,256]{2,1,0:T(8,128)(2,1)} %gather_fusion.1, pred[64]{0:T(512)(128)(4,1)S(1)} %get-tuple-element.468, bf16[192,128,128]{2,1,0:T(8,128)(2,1)} %get-tuple-element.529, s32[]{:T(128)S(6)} %select_n.107), kind=kOutput, calls=%fused_computation.32.clone.1 | convolution fusion | flops 538968064 | bytes 10485828 | tf_op jit(solution)/shard_map/while/body/eval_jaxpr/bij,bjk->bik/dot_general | solution.py:24
  392.0 0.1 dynamic_slice.63
  392.1 14.6 %select_add_fusion.5 = f32[96,128,256]{2,0,1:T(8,128)} fusion(f32[96,128,256]{2,0,1:T(8,128)} %get-tuple-element.515, pred[]{:T(512)S(6)} %compare.7, bf16[64,128,256]{2,1,0:T(8,128)(2,1)} %fusion.72, s32[64]{0:T(128)S(1)} %dynamic_slice.63, pred[64]{0:T(512)(128)(4,1)S(1)} %get-tuple-element.469), kind=kOutput, calls=%fused_computation.29.clone.1 | convolution fusion | flops 408963072 | bytes 29360448 | tf_op jit(solution)/shard_map/while/body/eval_jaxpr/gb,bik->gik/dot_general | solution.py:29
  406.8 0.7 compare_and_fusion.6
  407.5 5.6 %gather_fusion.1 = bf16[64,128,256]{2,1,0:T(8,128)(2,1)} fusion(bf16[96,128,256]{2,1,0:T(8,128)(2,1)} %get-tuple-element.531, s32[1024]{0:T(1024)S(1)} %pad_clamp_fusion.6), kind=kCustom, calls=%fused_computation.1.clone.clone.1 | custom fusion | bytes 8388864 | tf_op jit(solution)/shard_map/while/body/eval_jaxpr/jit(_take)/gather | solution.py:23
  413.1 6.2 %fusion.72 = bf16[64,128,256]{2,1,0:T(8,128)(2,1)} fusion(bf16[64,128,256]{2,1,0:T(8,128)(2,1)} %gather_fusion.1, pred[64]{0:T(512)(128)(4,1)S(1)} %get-tuple-element.468, bf16[192,128,128]{2,1,0:T(8,128)(2,1)} %get-tuple-element.529, s32[]{:T(128)S(6)} %select_n.107), kind=kOutput, calls=%fused_computation.32.clone.1 | convolution fusion | flops 538968064 | bytes 10485828 | tf_op jit(solution)/shard_map/while/body/eval_jaxpr/bij,bjk->bik/dot_general | solution.py:24
  419.3 0.1 dynamic_slice.63
  419.4 14.6 %select_add_fusion.5 = f32[96,128,256]{2,0,1:T(8,128)} fusion(f32[96,128,256]{2,0,1:T(8,128)} %get-tuple-element.515, pred[]{:T(512)S(6)} %compare.7, bf16[64,128,256]{2,1,0:T(8,128)(2,1)} %fusion.72, s32[64]{0:T(128)S(1)} %dynamic_slice.63, pred[64]{0:T(512)(128)(4,1)S(1)} %get-tuple-element.469), kind=kOutput, calls=%fused_computation.29.clone.1 | convolution fusion | flops 408963072 | bytes 29360448 | tf_op jit(solution)/shard_map/while/body/eval_jaxpr/gb,bik->gik/dot_general | solution.py:29
  434.0 13.9 %copy.23 = bf16[96,128,256]{2,1,0:T(8,128)(2,1)} copy(f32[96,128,256]{2,0,1:T(8,128)} %get-tuple-element.285) | data formatting | bytes 18874368 | tf_op jit(solution)/shard_map/while | solution.py:32
  447.9 74.6 %reduce-scatter.5.cloned.1.call-done = bf16[768,256]{1,0:T(8,128)(2,1)} async-done(((bf16[12288,256]{1,0:T(8,128)(2,1)}), bf16[768,256]{1,0:T(8,128)(2,1)}) %reduce-scatter.5.cloned.1.call-update) | async-done | bytes 393232 | tf_op jit(solution)/shard_map/reduce_scatter | solution.py:63
  522.5 2.0 fusion.47
  (26 shorter events, 0.1 us)
Async XLA Ops:
  6.5 1.5 copy-start
  6.5 54.4 %copy-start.5 = (s32[1,1,192]{2,1,0:T(1,128)S(1)}, s32[1,1,192]{2,1,0:T(1,128)}, u32[]{:S(2)}) copy-start(s32[1,1,192]{2,1,0:T(1,128)} %param.16) | copy-start | bytes 2308
  6.5 54.4 %copy-start.4 = (s32[1,1,192]{2,1,0:T(1,128)S(1)}, s32[1,1,192]{2,1,0:T(1,128)}, u32[]{:S(2)}) copy-start(s32[1,1,192]{2,1,0:T(1,128)} %param.17) | copy-start | bytes 2308
  6.5 54.4 %all-gather.3.cloned.1.call-start = ((), (), s32[]{:S(2)}) async-start(), calls=%async_computation.2 | async-start | bytes 6684672 | tf_op jit(solution)/shard_map/all_gather | solution.py:49
  11.6 250.9 %reduce-scatter.3.cloned.1.call-start = ((), (), s32[]{:S(2)}) async-start(), calls=%async_computation.3 | async-start | bytes 6684672 | tf_op jit(solution)/shard_map/reduce_scatter | solution.py:53
  153.0 109.5 %copy-start.2 = (bf16[256,256]{1,0:T(8,128)(2,1)S(1)}, bf16[256,256]{1,0:T(8,128)(2,1)}, u32[]{:S(2)}) copy-start(bf16[256,256]{1,0:T(8,128)(2,1)} %param.20) | copy-start | bytes 393220
  153.0 202.9 %all-gather.5.cloned.1.call-start = ((), (), s32[]{:S(2)}) async-start(), calls=%async_computation.4 | async-start | bytes 6684672 | tf_op jit(solution)/shard_map/all_gather | solution.py:59
  264.6 257.9 %reduce-scatter.5.cloned.1.call-start = ((), (), s32[]{:S(2)}) async-start(), calls=%async_computation.5 | async-start | bytes 6684672 | tf_op jit(solution)/shard_map/reduce_scatter | solution.py:63
  434.0 90.5 %copy-start.1 = (bf16[768,256]{1,0:T(8,128)(2,1)S(1)}, bf16[768,256]{1,0:T(8,128)(2,1)}, u32[]{:S(2)}) copy-start(bf16[768,256]{1,0:T(8,128)(2,1)} %param.14) | copy-start | bytes 1179652
  447.9 74.6 %copy-start.3 = (bf16[256,256]{1,0:T(8,128)(2,1)S(1)}, bf16[256,256]{1,0:T(8,128)(2,1)}, u32[]{:S(2)}) copy-start(bf16[256,256]{1,0:T(8,128)(2,1)} %param.21) | copy-start | bytes 393220
Sparse Core Ops, SparseCore 0:
  11.8 49.1 all-gather.2
  153.2 109.3 reduce-scatter.2
  265.0 90.9 all-gather.4
  448.1 74.4 reduce-scatter.4
where the time goes:
time: 535 us; the launch traced here: 531 us
  waiting for transfers between devices  325 us (61%)
  matrix products  122 us (23%)
  local copies, waits for them, and re-layouts  64.6 us (12%)
  between operations  13.2 us (2%)
  other arithmetic  6.76 us (1%)
    reduce_scatter x1, waiting for transfers between devices, on_device(): lax.psum_scatter(partial_one.astype(jnp.bfloat16), 'row', scatter_dimensi...  109 us
    all_gather x1, waiting for transfers between devices, on_device(): col_panel = lax.all_gather(hidden, 'row', axis=0, tiled=True)  91.3 us
    dot_general x6, matrix products, accumulate(): return carried + jnp.einsum('gb,bik->gik', selector, product)  80.5 us
    reduce_scatter x1, waiting for transfers between devices, on_device(): lax.psum_scatter(partial_two.astype(jnp.bfloat16), 'col', scatter_dimensi...  74.6 us
    all_gather x1, waiting for transfers between devices, on_device(): row_panel = lax.all_gather(initial, 'col', axis=0, tiled=True)  49.3 us
    dot_general x6, matrix products, accumulate(): jnp.einsum(pattern, blocks_now, chosen, preferred_element_type=jnp.float32)  37.2 us
    gather x6, local copies, waits for them, and re-layouts, accumulate(): chosen = jnp.take(tile_set, source_now, axis=0)  33.7 us
    while x2, local copies, waits for them, and re-layouts, block_product(): lax.fori_loop(0, rounds, accumulate, jnp.zeros((out_blocks, block_size, f...  27.7 us
  transfers between devices with their start and end apart: 4, of which 4 were waited for; matrix products, arithmetic and copies ran while one was open for 0% of the time, Pallas kernels for 0%

commit v1 on v0

v1 whole, which is shorter than its diff:
```python
import functools
import jax
import jax.numpy as jnp
from jax import lax
from jax.experimental import pallas as pl
from jax.experimental.pallas import tpu as pltpu
from jax.sharding import PartitionSpec as P

CHUNK = 16


def product_kernel(
    transposed, unroll, source_ref, target_ref, count_ref, panel_hbm, tile_hbm, out_hbm,
    tiles, panel, total, tile_sem, panel_sem, out_sem,
):
    slots, block = tile_hbm.shape[0], tile_hbm.shape[1]
    blocks = panel_hbm.shape[0]
    chunks = slots // CHUNK
    live = count_ref[0, 0]

    def tile_copy(c):
        part = pl.ds(c * CHUNK, CHUNK)
        return pltpu.make_async_copy(tile_hbm.at[part], tiles.at[part], tile_sem.at[c])

    panel_copy = pltpu.make_async_copy(panel_hbm, panel, panel_sem)
    panel_copy.start()
    for c in range(chunks):
        pl.when(c * CHUNK < live)(lambda c=c: tile_copy(c).start())

    @pl.loop(0, blocks)
    def _(g):
        total[g] = jnp.zeros_like(total[g])

    panel_copy.wait()
    dims = (((0,), (0,)), ((), ())) if transposed else (((1,), (0,)), ((), ()))

    def one_chunk(c):
        tile_copy(c).wait()

        @pl.loop(0, CHUNK // unroll)
        def _(step):
            first = c * CHUNK + step * unroll

            @pl.when(first < live)
            def _():
                products, targets = [], []
                for k in range(unroll):
                    slot = first + k
                    products.append(lax.dot_general(
                        tiles[slot], panel[source_ref[0, slot]], dims,
                        preferred_element_type=jnp.float32,
                    ))
                    targets.append(jnp.where(slot < live, target_ref[0, slot], blocks))
                for k in range(unroll):
                    total[targets[k]] += products[k]

    for c in range(chunks):
        pl.when(c * CHUNK < live)(functools.partial(one_chunk, c))

    rounds = 12
    share = blocks // rounds
    copies = []
    for c in range(rounds):
        @pl.loop(c * share, (c + 1) * share)
        def _(g):
            panel[g] = total[g].astype(panel.dtype)
        part = pl.ds(c * share, share)
        copies.append(pltpu.make_async_copy(panel.at[part], out_hbm.at[part], out_sem.at[c]))
        copies[-1].start()
    for copy in copies:
        copy.wait()


def block_product(panel, tiles, source_ids, target_ids, count, transposed, unroll=8):
    slots, block, _ = tiles.shape
    blocks, _, width = panel.shape
    smem = pl.BlockSpec(memory_space=pltpu.SMEM)
    hbm = pl.BlockSpec(memory_space=pl.ANY)
    return pl.pallas_call(
        functools.partial(product_kernel, transposed, unroll),
        out_shape=jax.ShapeDtypeStruct(panel.shape, panel.dtype),
        in_specs=[smem, smem, smem, hbm, hbm],
        out_specs=hbm,
        scratch_shapes=[
            pltpu.VMEM(tiles.shape, tiles.dtype),
            pltpu.VMEM(panel.shape, panel.dtype),
            pltpu.VMEM((blocks + 1, block, width), jnp.float32),
            pltpu.SemaphoreType.DMA((slots // CHUNK,)),
            pltpu.SemaphoreType.DMA,
            pltpu.SemaphoreType.DMA((12,)),
        ],
        compiler_params=pltpu.CompilerParams(vmem_limit_bytes=48 << 20),
        cost_estimate=pl.CostEstimate(
            flops=2 * slots * block * block * width, transcendentals=0,
            bytes_accessed=2 * (tiles.size + 2 * panel.size),
        ),
    )(source_ids, target_ids, count, panel, tiles)


def on_device(
    features, node_order, block_rows, block_cols, block_counts, adjacency, weight_one, weight_two
):
    initial = jnp.take(features, node_order[0], axis=0)
    tiles = adjacency[0, 0]
    rows, cols = block_rows[0], block_cols[0]
    block, width = tiles.shape[-1], features.shape[1]
    row_panel = lax.all_gather(initial, "col", axis=0, tiled=True)
    partial_one = block_product(
        row_panel.reshape(-1, block, width), tiles, rows, cols, block_counts, True
    )
    summed = lax.psum_scatter(
        partial_one.reshape(-1, width), "row", scatter_dimension=0, tiled=True
    )
    hidden = jax.nn.relu(jnp.dot(summed, weight_one, preferred_element_type=jnp.float32)).astype(
        jnp.bfloat16
    )
    col_panel = lax.all_gather(hidden, "row", axis=0, tiled=True)
    partial_two = block_product(
        col_panel.reshape(-1, block, width), tiles, cols, rows, block_counts, False
    )
    second = lax.psum_scatter(
        partial_two.reshape(-1, width), "col", scatter_dimension=0, tiled=True
    )
    return jax.nn.relu(jnp.dot(second, weight_two, preferred_element_type=jnp.float32)).astype(
        jnp.bfloat16
    )


def solution(mesh):
    in_specs = (
        P(("row", "col"), None),
        P(("row", "col"), None),
        P("row", "col", None),
        P("row", "col", None),
        P("row", "col"),
        P("row", "col", None, None, None),
        P(),
        P(),
    )
    out_specs = P(("row", "col"), None)
    return jax.shard_map(
        on_device, mesh=mesh, in_specs=in_specs, out_specs=out_specs, check_vma=False
    )
```

time: 535 us -> 381 us (0.71)
  matrix products: 122 us -> 4 us
  local copies, waits for them, and re-layouts: 64.6 us -> 4.04 us
  Pallas kernels: 0 us -> 16.9 us
  waiting for transfers between devices: 325 us -> 336 us
    dot_general x12 -> x0, matrix products: 118 us -> none  [the longest x6 80.5 us: accumulate(): return carried + jnp.einsum('gb,bik->gik', selector, product)]
    gather x6 -> x0, local copies, waits for them, and re-layouts: 33.7 us -> none  [accumulate(): chosen = jnp.take(tile_set, source_now, axis=0)]
    while x2 -> x0, local copies, waits for them, and re-layouts: 27.7 us -> none  [block_product(): lax.fori_loop(0, rounds, accumulate, jnp.zeros((out_blocks, block_size, f...]
    pallas_call x0 -> x2, Pallas kernels: none -> 16.9 us  [block_product(): pl.pallas_call(functools.partial(product_kernel, transposed, unroll), out...]
    reduce_scatter x2, waiting for transfers between devices: 184 us -> 196 us  [the longest x1 115 us: on_device(): lax.psum_scatter(partial_one.reshape(-1, width), 'row', scatter_dimension...]
where the time goes in v1:
time: 381 us; the launch traced here: 378 us
  waiting for transfers between devices  336 us (88%)
  Pallas kernels  16.9 us (4%)
  between operations  13.9 us (4%)
  local copies, waits for them, and re-layouts  4.04 us (1%)
  matrix products  4 us (1%)
    reduce_scatter x1, waiting for transfers between devices, on_device(): lax.psum_scatter(partial_one.reshape(-1, width), 'row', scatter_dimension...  115 us
    all_gather x1, waiting for transfers between devices, on_device(): col_panel = lax.all_gather(hidden, 'row', axis=0, tiled=True)  91.3 us
    reduce_scatter x1, waiting for transfers between devices, on_device(): lax.psum_scatter(partial_two.reshape(-1, width), 'col', scatter_dimension...  81.2 us
    all_gather x1, waiting for transfers between devices, on_device(): row_panel = lax.all_gather(initial, 'col', axis=0, tiled=True)  48.6 us
    pallas_call x2, Pallas kernels, block_product(): pl.pallas_call(functools.partial(product_kernel, transposed, unroll), out...  16.9 us
  transfers between devices with their start and end apart: 4, of which 4 were waited for; matrix products, arithmetic and copies ran while one was open for 0% of the time, Pallas kernels for 0%

profile of v1, /device:TPU:1, one launch (start us, length us, event | category | flops | bytes accessed | tf_op | source)
XLA Modules:
  0.0 377.5 jit_solution(14862080419701716303)
XLA Ops:
  6.5 0.0 copy-start
  6.5 0.0 all-gather.3.cloned.1.call-start
  6.5 0.7 fusion.2
  7.3 0.7 reduce
  8.0 0.0 copy-done
  8.0 2.7 gather_fusion
  10.7 0.9 broadcast_select_fusion
  11.6 0.0 all-gather.3.cloned.1.call-update
  11.6 0.0 reduce-scatter.3.cloned.1.call-start
  12.3 48.6 %all-gather.3.cloned.1.call-done = bf16[12288,256]{1,0:T(8,128)(2,1)} async-done(((bf16[768,256]{1,0:T(8,128)(2,1)}), bf16[12288,256]{1,0:T(8,128)(2,1)}) %all-gather.3.cloned.1.call-update) | async-done | bytes 6291472 | tf_op jit(solution)/shard_map/all_gather | solution.py:107
  61.0 0.0 copy-start.1
  61.0 0.7 copy-done.1
  61.6 0.0 copy-start.3
  61.6 0.7 copy-done.3
  62.3 8.5 %shard_map.82 = bf16[96,128,256]{2,1,0:T(8,128)(2,1)} custom-call(s32[1,192]{1,0:T(1,128)S(1)} %bitcast.13, s32[1,192]{1,0:T(1,128)S(1)} %bitcast.15, s32[1,1]{1,0:T(1,128)S(6)} %copy.9.count_ref, bf16[96,128,256]{2,1,0:T(8,128)(2,1)} %bitcast.21, bf16[192,128,128]{2,1,0:T(8,128)(2,1)} %bitcast.19), custom_call_target="tpu_custom_call" | custom-call | flops 1610612736 | bytes 18874368 | tf_op jit(solution)/shard_map/pallas_call | solution.py:79
  70.9 0.0 copy-start.5
  70.9 0.0 copy-start.2
  70.9 0.0 copy-start.4
  70.9 0.0 reduce-scatter.3.cloned.1.call-update
  70.9 0.0 all-gather.5.cloned.1.call-start
  71.0 115.0 %reduce-scatter.3.cloned.1.call-done = bf16[768,256]{1,0:T(8,128)(2,1)} async-done(((bf16[12288,256]{1,0:T(8,128)(2,1)}), bf16[768,256]{1,0:T(8,128)(2,1)}) %reduce-scatter.3.cloned.1.call-update) | async-done | bytes 393232 | tf_op jit(solution)/shard_map/reduce_scatter | solution.py:111
  186.0 0.0 copy-done.5
  186.0 2.0 fusion
  188.0 0.0 all-gather.5.cloned.1.call-update
  188.0 0.0 reduce-scatter.5.cloned.1.call-start
  188.1 91.3 %all-gather.5.cloned.1.call-done = bf16[12288,256]{1,0:T(8,128)(2,1)} async-done(((bf16[768,256]{1,0:T(8,128)(2,1)}), bf16[12288,256]{1,0:T(8,128)(2,1)}) %all-gather.5.cloned.1.call-update) | async-done | bytes 6291472 | tf_op jit(solution)/shard_map/all_gather | solution.py:117
  279.4 0.0 copy-done.2
  279.4 0.0 copy-done.4
  279.4 8.4 %shard_map.83 = bf16[96,128,256]{2,1,0:T(8,128)(2,1)} custom-call(s32[1,192]{1,0:T(1,128)S(1)} %bitcast.16, s32[1,192]{1,0:T(1,128)S(1)} %bitcast.14, s32[1,1]{1,0:T(1,128)S(6)} %copy.9.count_ref, bf16[96,128,256]{2,1,0:T(8,128)(2,1)} %bitcast.22, bf16[192,128,128]{2,1,0:T(8,128)(2,1)} %bitcast.20), custom_call_target="tpu_custom_call" | custom-call | flops 1610612736 | bytes 18874368 | tf_op jit(solution)/shard_map/pallas_call | solution.py:79
  287.8 0.0 copy-start.6
  287.8 0.0 reduce-scatter.5.cloned.1.call-update
  287.8 81.2 %reduce-scatter.5.cloned.1.call-done = bf16[768,256]{1,0:T(8,128)(2,1)} async-done(((bf16[12288,256]{1,0:T(8,128)(2,1)}), bf16[768,256]{1,0:T(8,128)(2,1)}) %reduce-scatter.5.cloned.1.call-update) | async-done | bytes 393232 | tf_op jit(solution)/shard_map/reduce_scatter | solution.py:121
  369.0 0.0 copy-done.6
  369.0 2.0 fusion.1
  (2 shorter events, 0.0 us)
Async XLA Ops:
  6.5 1.5 copy-start
  6.5 54.4 %all-gather.3.cloned.1.call-start = ((), (), s32[]{:S(2)}) async-start(), calls=%async_computation.2 | async-start | bytes 6684672 | tf_op jit(solution)/shard_map/all_gather | solution.py:107
  11.6 174.3 %reduce-scatter.3.cloned.1.call-start = ((), (), s32[]{:S(2)}) async-start(), calls=%async_computation.3 | async-start | bytes 6684672 | tf_op jit(solution)/shard_map/reduce_scatter | solution.py:111
  61.0 0.7 copy-start.1
  61.6 0.7 copy-start.3
  70.9 115.1 %copy-start.5 = (bf16[256,256]{1,0:T(8,128)(2,1)S(1)}, bf16[256,256]{1,0:T(8,128)(2,1)}, u32[]{:S(2)}) copy-start(bf16[256,256]{1,0:T(8,128)(2,1)} %param.14) | copy-start | bytes 393220
  70.9 208.5 %copy-start.2 = (s32[1,1,192]{2,1,0:T(1,128)S(1)}, s32[1,1,192]{2,1,0:T(1,128)}, u32[]{:S(2)}) copy-start(s32[1,1,192]{2,1,0:T(1,128)} %param.10) | copy-start | bytes 2308
  70.9 208.5 %copy-start.4 = (s32[1,1,192]{2,1,0:T(1,128)S(1)}, s32[1,1,192]{2,1,0:T(1,128)}, u32[]{:S(2)}) copy-start(s32[1,1,192]{2,1,0:T(1,128)} %param.11) | copy-start | bytes 2308
  70.9 208.5 %all-gather.5.cloned.1.call-start = ((), (), s32[]{:S(2)}) async-start(), calls=%async_computation.4 | async-start | bytes 6684672 | tf_op jit(solution)/shard_map/all_gather | solution.py:117
  188.0 181.0 %reduce-scatter.5.cloned.1.call-start = ((), (), s32[]{:S(2)}) async-start(), calls=%async_computation.5 | async-start | bytes 6684672 | tf_op jit(solution)/shard_map/reduce_scatter | solution.py:121
  287.8 81.2 %copy-start.6 = (bf16[256,256]{1,0:T(8,128)(2,1)S(1)}, bf16[256,256]{1,0:T(8,128)(2,1)}, u32[]{:S(2)}) copy-start(bf16[256,256]{1,0:T(8,128)(2,1)} %param.15) | copy-start | bytes 393220
Sparse Core Ops, SparseCore 0:
  11.8 49.1 all-gather.2
  71.1 114.8 reduce-scatter.2
  188.4 90.9 all-gather.4
  287.9 81.0 reduce-scatter.4

commit v2 on v1

--- a/solution.py
+++ b/solution.py
@@ -5,6 +5,382 @@
 from jax.experimental import pallas as pl
 from jax.experimental.pallas import tpu as pltpu
 from jax.sharding import PartitionSpec as P
+
+MESH = pl.DeviceIdType.MESH
+PARTS = 3
+
+
+class Mail:
+    def __init__(self, send_sem, recv_sem):
+        self.send_sem, self.recv_sem, self.sent = send_sem, recv_sem, {}
+
+    def send(self, name, src, dst, device):
+        slot = len(self.sent)
+        copy = pltpu.make_async_remote_copy(
+            src_ref=src, dst_ref=dst, send_sem=self.send_sem.at[slot],
+            recv_sem=self.recv_sem.at[slot], device_id=device, device_id_type=MESH,
+        )
+        copy.start()
+        self.sent[name] = copy
+
+    def await_recv(self, *names):
+        for name in names:
+            self.sent[name].wait_recv()
+
+    def finish(self):
+        for copy in self.sent.values():
+            copy.wait_send()
+
+
+def greet(devices):
+    barrier = pltpu.get_barrier_semaphore()
+    for device in devices:
+        pl.semaphore_signal(barrier, inc=1, device_id=device, device_id_type=MESH)
+    pl.semaphore_wait(barrier, len(devices))
+
+
+def add_rows(out, terms):
+    rows = out.shape[0]
+    step = next(s for s in (64, 48, 32, 16) if rows % s == 0)
+
+    @pl.loop(0, rows // step)
+    def _(i):
+        at = pl.ds(pl.multiple_of(i * step, step), step)
+        total = terms[0][at].astype(jnp.float32)
+        for term in terms[1:]:
+            total += term[at].astype(jnp.float32)
+        out[at] = total.astype(out.dtype)
+
+
+def dense_relu(out, terms, weight):
+    total = terms[0][...].astype(jnp.float32)
+    for term in terms[1:]:
+        total += term[...].astype(jnp.float32)
+    product = jnp.dot(total.astype(jnp.bfloat16), weight[...], preferred_element_type=jnp.float32)
+    out[...] = jnp.maximum(product, 0.0).astype(out.dtype)
+
+
+def row_kernel(
+    part, weight, out, own_r, own_l, own_m, x1_l, x1_r, x2_l, x2_r, x3_l, x3_r, xc_r, xc_l, sx,
+    z1_l, z1_r, z2_l, z2_r, z3_l, z3_r, zc_r, zc_l, hid, send_sem, recv_sem, local_sem, hid_sem,
+):
+    slab = part.shape[2]
+    n = slab // PARTS
+    h = n // 2
+    me = lax.axis_index("row")
+    z, x = me // 4, me % 4
+    xr, xl, xo = (x + 1) % 4, (x + 3) % 4, (x + 2) % 4
+    zr, zl, zo = (z + 1) % 4, (z + 3) % 4, (z + 2) % 4
+    to_xr, to_xl = {"row": z * 4 + xr}, {"row": z * 4 + xl}
+    to_zr, to_zl = {"row": zr * 4 + x}, {"row": zl * 4 + x}
+    loads = [
+        pltpu.make_async_copy(part.at[:, at], own, local_sem.at[i])
+        for i, (at, own) in enumerate(((xr, own_r), (xl, own_l), (x, own_m)))
+    ]
+    for load in loads:
+        load.start()
+    greet((to_xr, to_xl, to_zr, to_zl))
+    mail = Mail(send_sem, recv_sem)
+
+    def half(p, k):
+        return pl.ds(p * n + k * h, h)
+
+    def x12(p):
+        a, b = half(p, 0), half(p, 1)
+        mail.send(("x1r", p), part.at[:, xo, a], x1_l.at[p], to_xr)
+        mail.send(("x1l", p), part.at[:, xo, b], x1_r.at[p], to_xl)
+        mail.send(("x2r", p), part.at[:, xr, b], x2_l.at[p], to_xr)
+        mail.send(("x2l", p), part.at[:, xl, a], x2_r.at[p], to_xl)
+
+    def x3(p):
+        a, b = half(p, 0), half(p, 1)
+        if p == 0:
+            loads[0].wait()
+            loads[1].wait()
+        mail.await_recv(("x1r", p))
+        for k in range(4):
+            add_rows(xc_r.at[p, k], (x1_l.at[p, k], own_r.at[k, a]))
+        mail.send(("x3r", p), xc_r.at[p], x3_l.at[p], to_xr)
+        mail.await_recv(("x1l", p))
+        for k in range(4):
+            add_rows(xc_l.at[p, k], (x1_r.at[p, k], own_l.at[k, b]))
+        mail.send(("x3l", p), xc_l.at[p], x3_r.at[p], to_xl)
+
+    def x4(p):
+        a, b = half(p, 0), half(p, 1)
+        if p == 0:
+            loads[2].wait()
+        mail.await_recv(("x2l", p), ("x3r", p))
+        for k in range(4):
+            add_rows(sx.at[p, 0, k], (own_m.at[k, a], x3_l.at[p, k], x2_r.at[p, k]))
+        mail.send(("z1r", p), sx.at[p, 0, zo], z1_l.at[p], to_zr)
+        mail.send(("z2l", p), sx.at[p, 0, zl], z2_r.at[p], to_zl)
+        mail.await_recv(("x2r", p), ("x3l", p))
+        for k in range(4):
+            add_rows(sx.at[p, 1, k], (own_m.at[k, b], x3_r.at[p, k], x2_l.at[p, k]))
+        mail.send(("z1l", p), sx.at[p, 1, zo], z1_r.at[p], to_zl)
+        mail.send(("z2r", p), sx.at[p, 1, zr], z2_l.at[p], to_zr)
+
+    def z3(p):
+        mail.await_recv(("z1r", p))
+        add_rows(zc_r.at[p], (z1_l.at[p], sx.at[p, 0, zr]))
+        mail.send(("z3r", p), zc_r.at[p], z3_l.at[p], to_zr)
+        mail.await_recv(("z1l", p))
+        add_rows(zc_l.at[p], (z1_r.at[p], sx.at[p, 1, zl]))
+        mail.send(("z3l", p), zc_l.at[p], z3_r.at[p], to_zl)
+
+    def z4(p):
+        a, b = half(p, 0), half(p, 1)
+        mail.await_recv(("z2l", p), ("z3r", p))
+        dense_relu(hid.at[a], (sx.at[p, 0, z], z3_l.at[p], z2_r.at[p]), weight)
+        mail.await_recv(("z2r", p), ("z3l", p))
+        dense_relu(hid.at[b], (sx.at[p, 1, z], z3_r.at[p], z2_l.at[p]), weight)
+        mail.send(("g1ar", p), hid.at[a], out.at[z, x, a], to_zr)
+        mail.send(("g1bl", p), hid.at[b], out.at[z, x, b], to_zl)
+        mail.send(("g1br", p), hid.at[b], out.at[z, x, b], to_zr)
+        mail.send(("g1al", p), hid.at[a], out.at[z, x, a], to_zl)
+        whole = pl.ds(p * n, n)
+        pltpu.make_async_copy(hid.at[whole], out.at[z, x, whole], hid_sem.at[p]).start()
+
+    def g2(p):
+        a, b = half(p, 0), half(p, 1)
+        mail.await_recv(("g1ar", p))
+        mail.send(("g2r", p), out.at[zl, x, a], out.at[zl, x, a], to_zr)
+        mail.await_recv(("g1bl", p))
+        mail.send(("g2l", p), out.at[zr, x, b], out.at[zr, x, b], to_zl)
+
+    def g3(p):
+        a, b = half(p, 0), half(p, 1)
+        mail.await_recv(("g1br", p), ("g1al", p), ("g2r", p), ("g2l", p))
+        whole = pl.ds(p * n, n)
+        pltpu.make_async_copy(hid.at[whole], out.at[z, x, whole], hid_sem.at[p]).wait()
+        for name, rows, to in (("g3ar", a, to_xr), ("g3bl", b, to_xl), ("g3br", b, to_xr), ("g3al", a, to_xl)):
+            mail.send((name, p), out.at[:, x, rows], out.at[:, x, rows], to)
+
+    def g4(p):
+        a, b = half(p, 0), half(p, 1)
+        mail.await_recv(("g3ar", p))
+        mail.send(("g4r", p), out.at[:, xl, a], out.at[:, xl, a], to_xr)
+        mail.await_recv(("g3bl", p))
+        mail.send(("g4l", p), out.at[:, xr, b], out.at[:, xr, b], to_xl)
+
+    def g5(p):
+        mail.await_recv(("g3br", p), ("g3al", p), ("g4r", p), ("g4l", p))
+
+    stages = ((x12, 0), (x3, 1), (x4, 2), (z3, 3), (z4, 4), (g2, 5), (g3, 6), (g4, 7), (g5, 8))
+    for tick in range(PARTS + len(stages) - 1):
+        for stage, lag in stages:
+            if 0 <= tick - lag < PARTS:
+                stage(tick - lag)
+    mail.finish()
+
+
+def row_exchange(part, weight):
+    _, slab, width = part.shape
+    h = slab // PARTS // 2
+    dt = part.dtype
+    hbm = pl.BlockSpec(memory_space=pl.ANY)
+    count = 24 * PARTS
+    out = pl.pallas_call(
+        row_kernel,
+        out_shape=jax.ShapeDtypeStruct((4, 4, slab, width), dt),
+        in_specs=[hbm, pl.BlockSpec(memory_space=pltpu.VMEM)],
+        out_specs=hbm,
+        scratch_shapes=(
+            [pltpu.VMEM((4, slab, width), dt)] * 3
+            + [pltpu.VMEM((PARTS, 4, h, width), dt)] * 8
+            + [pltpu.VMEM((PARTS, 2, 4, h, width), dt)]
+            + [pltpu.VMEM((PARTS, h, width), dt)] * 8
+            + [pltpu.VMEM((slab, width), dt)]
+            + [pltpu.SemaphoreType.DMA((count,))] * 2
+            + [pltpu.SemaphoreType.DMA((3,)), pltpu.SemaphoreType.DMA((PARTS,))]
+        ),
+        compiler_params=pltpu.CompilerParams(
+            collective_id=1, has_side_effects=True, vmem_limit_bytes=60 << 20
+        ),
+    )(part.reshape(4, 4, slab, width), weight)
+    return out.reshape(16, slab, width)
+
+
+def gather_kernel(order, features, out, own, send_sem, recv_sem, own_sem):
+    slab = features.shape[0]
+    h = slab // 2
+    me = lax.axis_index("col")
+    zp, y, c = me // 8, (me // 2) % 4, me % 2
+    yr, yl, yo, zq = (y + 1) % 4, (y + 3) % 4, (y + 2) % 4, 1 - zp
+    to_r, to_l = {"col": zp * 8 + yr * 2 + c}, {"col": zp * 8 + yl * 2 + c}
+    to_z, to_c = {"col": zq * 8 + y * 2 + c}, {"col": zp * 8 + y * 2 + 1 - c}
+    step = 128 if h % 128 == 0 else h
+
+    def place(half):
+        @pl.loop(0, h // step)
+        def _(i):
+            at = pl.ds(pl.multiple_of(half * h + i * step, step), step)
+            place_of = order[:, at]
+            chosen = lax.broadcasted_iota(jnp.int32, (slab, step), 0) == place_of
+            own[at] = lax.dot_general(
+                chosen.astype(features.dtype), features[...], (((0,), (0,)), ((), ())),
+                preferred_element_type=jnp.float32,
+            ).astype(own.dtype)
+
+    place(0)
+    greet((to_r, to_l, to_z, to_c))
+    mail = Mail(send_sem, recv_sem)
+    a, b, whole = pl.ds(0, h), pl.ds(h, h), pl.ds(0, slab)
+
+    def send_own(name, rows, to):
+        mail.send(name, own.at[rows], out.at[zp, y, c, rows], to)
+
+    def send_on(name, zs, ys, rows, to):
+        mail.send(name, out.at[zs, ys, c, rows], out.at[zs, ys, c, rows], to)
+
+    send_own("ar", a, to_r)
+    send_own("za", a, to_z)
+    place(1)
+    send_own("bl", b, to_l)
+    send_own("zb", b, to_z)
+    send_own("br", b, to_r)
+    send_own("al", a, to_l)
+    send_own("c0", whole, to_c)
+    own_copy = pltpu.make_async_copy(own, out.at[zp, y, c], own_sem)
+    own_copy.start()
+    mail.await_recv("ar")
+    send_on("fr", zp, yl, a, to_r)
+    mail.await_recv("bl")
+    send_on("fl", zp, yr, b, to_l)
+    mail.await_recv("za")
+    send_on("par", zq, y, a, to_r)
+    send_on("pal", zq, y, a, to_l)
+    mail.await_recv("zb")
+    send_on("pbr", zq, y, b, to_r)
+    send_on("pbl", zq, y, b, to_l)
+    send_on("c1", zq, y, whole, to_c)
+    mail.await_recv("br")
+    send_on("c2", zp, yl, whole, to_c)
+    mail.await_recv("al")
+    send_on("c3", zp, yr, whole, to_c)
+    mail.await_recv("fr")
+    send_on("zoa", zp, yo, a, to_z)
+    mail.await_recv("fl")
+    send_on("zob", zp, yo, b, to_z)
+    send_on("c4", zp, yo, whole, to_c)
+    mail.await_recv("par", "pbr")
+    send_on("c5", zq, yl, whole, to_c)
+    mail.await_recv("pal", "pbl")
+    send_on("c6", zq, yr, whole, to_c)
+    mail.await_recv("zoa")
+    send_on("c7a", zq, yo, a, to_c)
+    mail.await_recv("zob")
+    send_on("c7b", zq, yo, b, to_c)
+    own_copy.wait()
+    mail.await_recv("c0", "c1", "c2", "c3", "c4", "c5", "c6", "c7a", "c7b")
+    mail.finish()
+
+
+def col_gather(order, features):
+    slab, width = features.shape
+    vmem = pl.BlockSpec(memory_space=pltpu.VMEM)
+    out = pl.pallas_call(
+        gather_kernel,
+        out_shape=jax.ShapeDtypeStruct((2, 4, 2, slab, width), features.dtype),
+        in_specs=[vmem, vmem],
+        out_specs=pl.BlockSpec(memory_space=pl.ANY),
+        scratch_shapes=[
+            pltpu.VMEM((slab, width), features.dtype),
+            pltpu.SemaphoreType.DMA((23,)),
+            pltpu.SemaphoreType.DMA((23,)),
+            pltpu.SemaphoreType.DMA,
+        ],
+        compiler_params=pltpu.CompilerParams(
+            collective_id=0, has_side_effects=True, vmem_limit_bytes=60 << 20
+        ),
+    )(order, features)
+    return out.reshape(16, slab, width)
+
+
+def sum_kernel(
+    part, weight, out, own, sib, both, z1, s2_l, s2_r, s3_l, s3_r, opp, s4b_l, s4b_r, s4a_l, s4a_r,
+    c_r, c_l, via, z2, send_sem, recv_sem, own_sem,
+):
+    slab = part.shape[3]
+    h = slab // 2
+    me = lax.axis_index("col")
+    zp, y, c = me // 8, (me // 2) % 4, me % 2
+    yr, yl, yo, zq, d = (y + 1) % 4, (y + 3) % 4, (y + 2) % 4, 1 - zp, 1 - c
+    to_r, to_l = {"col": zp * 8 + yr * 2 + c}, {"col": zp * 8 + yl * 2 + c}
+    to_z, to_c = {"col": zq * 8 + y * 2 + c}, {"col": zp * 8 + y * 2 + d}
+    a, b = pl.ds(0, h), pl.ds(h, h)
+    dests = ((zq, yo), (zq, yr), (zq, yl), (zp, yr), (zp, yl), (zp, yo), (zq, y), (zp, y))
+    loads = [
+        pltpu.make_async_copy(part.at[zs, ys, c], own.at[i], own_sem.at[i])
+        for i, (zs, ys) in enumerate(dests)
+    ]
+    for load in loads:
+        load.start()
+    greet((to_r, to_l, to_z, to_c))
+    mail = Mail(send_sem, recv_sem)
+    for i, (zs, ys) in enumerate(dests):
+        mail.send(("c", i), part.at[zs, ys, d], sib.at[i], to_c)
+
+    def join(i):
+        loads[i].wait()
+        mail.await_recv(("c", i))
+        add_rows(both.at[i], (own.at[i], sib.at[i]))
+
+    join(0)
+    mail.send("z1", both.at[0], z1, to_z)
+    join(1)
+    mail.send("s2r", both.at[1], s2_l, to_r)
+    join(2)
+    mail.send("s2l", both.at[2], s2_r, to_l)
+    join(3)
+    mail.send("s4br", both.at[3, b], s4b_l, to_r)
+    join(4)
+    mail.send("s4bl", both.at[4, a], s4b_r, to_l)
+    join(5)
+    mail.await_recv("z1")
+    add_rows(opp, (both.at[5], z1))
+    mail.send("s3r", opp.at[a], s3_l, to_r)
+    mail.send("s3l", opp.at[b], s3_r, to_l)
+    join(6)
+    join(7)
+    mail.await_recv("s2r", "s2l")
+    add_rows(via, (both.at[6], s2_l, s2_r))
+    mail.send("z2", via, z2, to_z)
+    mail.await_recv("s3r")
+    add_rows(c_r, (both.at[3, a], s3_l))
+    mail.send("s4ar", c_r, s4a_l, to_r)
+    mail.await_recv("s3l")
+    add_rows(c_l, (both.at[4, b], s3_r))
+    mail.send("s4al", c_l, s4a_r, to_l)
+    mail.await_recv("z2", "s4bl", "s4ar")
+    dense_relu(out.at[a], (both.at[7, a], s4a_l, s4b_r, z2.at[a]), weight)
+    mail.await_recv("s4br", "s4al")
+    dense_relu(out.at[b], (both.at[7, b], s4b_l, s4a_r, z2.at[b]), weight)
+    mail.finish()
+
+
+def col_sum(part, weight):
+    _, slab, width = part.shape
+    dt, h = part.dtype, slab // 2
+    vmem = pl.BlockSpec(memory_space=pltpu.VMEM)
+    full, half = pltpu.VMEM((slab, width), dt), pltpu.VMEM((h, width), dt)
+    return pl.pallas_call(
+        sum_kernel,
+        out_shape=jax.ShapeDtypeStruct((slab, width), dt),
+        in_specs=[pl.BlockSpec(memory_space=pl.ANY), vmem],
+        out_specs=vmem,
+        scratch_shapes=(
+            [pltpu.VMEM((8, slab, width), dt)] * 3
+            + [full] * 3 + [half] * 2 + [full] + [half] * 6 + [full] * 2
+            + [pltpu.SemaphoreType.DMA((18,))] * 2
+            + [pltpu.SemaphoreType.DMA((8,))]
+        ),
+        compiler_params=pltpu.CompilerParams(
+            collective_id=2, has_side_effects=True, vmem_limit_bytes=60 << 20
+        ),
+    )(part.reshape(2, 4, 2, slab, width), weight)
+
 
 CHUNK = 16
 
@@ -89,7 +465,7 @@
             pltpu.SemaphoreType.DMA,
             pltpu.SemaphoreType.DMA((12,)),
         ],
-        compiler_params=pltpu.CompilerParams(vmem_limit_bytes=48 << 20),
+        compiler_params=pltpu.CompilerParams(vmem_limit_bytes=60 << 20),
         cost_estimate=pl.CostEstimate(
             flops=2 * slots * block * block * width, transcendentals=0,
             bytes_accessed=2 * (tiles.size + 2 * panel.size),
@@ -100,30 +476,18 @@
 def on_device(
     features, node_order, block_rows, block_cols, block_counts, adjacency, weight_one, weight_two
 ):
-    initial = jnp.take(features, node_order[0], axis=0)
     tiles = adjacency[0, 0]
     rows, cols = block_rows[0], block_cols[0]
-    block, width = tiles.shape[-1], features.shape[1]
-    row_panel = lax.all_gather(initial, "col", axis=0, tiled=True)
+    block, (slab, width) = tiles.shape[-1], features.shape
+    row_panel = col_gather(node_order, features)
     partial_one = block_product(
         row_panel.reshape(-1, block, width), tiles, rows, cols, block_counts, True
     )
-    summed = lax.psum_scatter(
-        partial_one.reshape(-1, width), "row", scatter_dimension=0, tiled=True
-    )
-    hidden = jax.nn.relu(jnp.dot(summed, weight_one, preferred_element_type=jnp.float32)).astype(
-        jnp.bfloat16
-    )
-    col_panel = lax.all_gather(hidden, "row", axis=0, tiled=True)
+    col_panel = row_exchange(partial_one.reshape(-1, slab, width), weight_one)
     partial_two = block_product(
         col_panel.reshape(-1, block, width), tiles, cols, rows, block_counts, False
     )
-    second = lax.psum_scatter(
-        partial_two.reshape(-1, width), "col", scatter_dimension=0, tiled=True
-    )
-    return jax.nn.relu(jnp.dot(second, weight_two, preferred_element_type=jnp.float32)).astype(
-        jnp.bfloat16
-    )
+    return col_sum(partial_two.reshape(-1, slab, width), weight_two)
 
 
 def solution(mesh):

time: 381 us -> 244 us (0.64)
  waiting for transfers between devices: 336 us -> 0 us
  Pallas kernels: 16.9 us -> 240 us
  between operations: 13.9 us -> 0.69 us
  matrix products: 4 us -> 0 us
    pallas_call x0 -> x3, Pallas kernels: none -> 224 us  [the longest x1 152 us: row_exchange(): pl.pallas_call(row_kernel, out_shape=jax.ShapeDtypeStruct((4, 4, slab, wi...]
    reduce_scatter x2 -> x0, waiting for transfers between devices: 196 us -> none  [the longest x1 115 us: on_device(): lax.psum_scatter(partial_one.reshape(-1, width), 'row', scatter_dimension...]
    all_gather x2 -> x0, waiting for transfers between devices: 140 us -> none  [the longest x1 91.3 us: on_device(): col_panel = lax.all_gather(hidden, 'row', axis=0, tiled=True)]
    dot_general x2 -> x0, matrix products: 4 us -> none  [the longest x1 2 us: on_device(): jnp.dot(second, weight_two, preferred_element_type=jnp.float32)]
  transfers between devices with their start and end apart: 4 -> 0, of which waited for: 4 -> 0; matrix products, arithmetic and copies ran while one was open for 0% -> 0% of each run, Pallas kernels for 0% -> 0%
where the time goes in v2:
time: 244 us; the launch traced here: 242 us
  Pallas kernels  240 us (98%)
    pallas_call x1, Pallas kernels, row_exchange(): pl.pallas_call(row_kernel, out_shape=jax.ShapeDtypeStruct((4, 4, slab, wi...  152 us
    pallas_call x1, Pallas kernels, col_sum(): pl.pallas_call(sum_kernel, out_shape=jax.ShapeDtypeStruct((slab, width),...  38.3 us
    pallas_call x1, Pallas kernels, col_gather(): pl.pallas_call(gather_kernel, out_shape=jax.ShapeDtypeStruct((2, 4, 2, sl...  33.1 us
    pallas_call x2, Pallas kernels, block_product(): pl.pallas_call(functools.partial(product_kernel, transposed, unroll), out...  16.2 us

profile of v2, /device:TPU:1, one launch (start us, length us, event | category | flops | bytes accessed | tf_op | source)
XLA Modules:
  0.0 242.3 jit_solution(17687544868510443144)
XLA Ops:
  0.7 33.1 %shard_map.82 = bf16[2,4,2,768,256]{4,3,2,1,0:T(8,128)(2,1)} custom-call(s32[1,768]{1,0:T(1,128)} %order.1, bf16[768,256]{1,0:T(8,128)(2,1)} %features.1), custom_call_target="tpu_custom_call" | custom-call | tf_op jit(solution)/shard_map/pallas_call | solution.py:283
  33.7 8.2 %shard_map.83 = bf16[96,128,256]{2,1,0:T(8,128)(2,1)} custom-call(s32[1,192]{1,0:T(1,128)} %bitcast.15, s32[1,192]{1,0:T(1,128)} %bitcast.13, s32[1,1]{1,0:T(1,128)S(6)} %copy.10.count_ref, bf16[96,128,256]{2,1,0:T(8,128)(2,1)} %bitcast.12, bf16[192,128,128]{2,1,0:T(8,128)(2,1)} %bitcast.9), custom_call_target="tpu_custom_call" | custom-call | flops 1610612736 | bytes 18874368 | tf_op jit(solution)/shard_map/pallas_call | solution.py:455
  41.9 152.3 %shard_map.84 = bf16[4,4,768,256]{3,2,1,0:T(8,128)(2,1)} custom-call(bf16[4,4,768,256]{3,2,1,0:T(8,128)(2,1)} %bitcast.8, bf16[256,256]{1,0:T(8,128)(2,1)} %weight.2), custom_call_target="tpu_custom_call" | custom-call | tf_op jit(solution)/shard_map/pallas_call | solution.py:184
  194.3 8.0 %shard_map.85 = bf16[96,128,256]{2,1,0:T(8,128)(2,1)} custom-call(s32[1,192]{1,0:T(1,128)} %bitcast.14, s32[1,192]{1,0:T(1,128)} %bitcast.16, s32[1,1]{1,0:T(1,128)S(6)} %copy.10.count_ref, bf16[96,128,256]{2,1,0:T(8,128)(2,1)} %bitcast.7, bf16[192,128,128]{2,1,0:T(8,128)(2,1)} %bitcast.10), custom_call_target="tpu_custom_call" | custom-call | flops 1610612736 | bytes 18874368 | tf_op jit(solution)/shard_map/pallas_call | solution.py:455
  202.3 38.3 %shard_map.86 = bf16[768,256]{1,0:T(8,128)(2,1)} custom-call(bf16[2,4,2,768,256]{4,3,2,1,0:T(8,128)(2,1)} %bitcast.11, bf16[256,256]{1,0:T(8,128)(2,1)} %weight.3), custom_call_target="tpu_custom_call" | custom-call | tf_op jit(solution)/shard_map/pallas_call | solution.py:368
  240.6 1.8 copy.11

commit v3 on v2

--- a/solution.py
+++ b/solution.py
@@ -7,7 +7,8 @@
 from jax.sharding import PartitionSpec as P
 
 MESH = pl.DeviceIdType.MESH
-PARTS = 3
+PARTS = 4
+LAGS = dict(r1=0, r2=1, r3=2, r4=3, r5=4, d=5, g2=5, g4=6, g3=6, g3o=6, g5=8, g4o=14, end=15)
 
 
 class Mail:
@@ -61,10 +62,11 @@
 
 
 def row_kernel(
-    part, weight, out, own_r, own_l, own_m, x1_l, x1_r, x2_l, x2_r, x3_l, x3_r, xc_r, xc_l, sx,
-    z1_l, z1_r, z2_l, z2_r, z3_l, z3_r, zc_r, zc_l, hid, send_sem, recv_sem, local_sem, hid_sem,
+    part, weight, out, own, r1_l, r1_r, cz, r2_l, r2_r, r2o_l, r2o_r, cx_r, cx_l, r3m_l, r3m_r,
+    r3b_l, r3a_r, r3a_l, r3b_r, sx, r4_l, r4_r, r5b_l, r5a_r, r5a_l, r5b_r, cs_r, cs_l, hid,
+    send_sem, recv_sem, own_sem, hid_sem,
 ):
-    slab = part.shape[2]
+    slab = part.shape[3]
     n = slab // PARTS
     h = n // 2
     me = lax.axis_index("row")
@@ -73,132 +75,195 @@
     zr, zl, zo = (z + 1) % 4, (z + 3) % 4, (z + 2) % 4
     to_xr, to_xl = {"row": z * 4 + xr}, {"row": z * 4 + xl}
     to_zr, to_zl = {"row": zr * 4 + x}, {"row": zl * 4 + x}
+    same, other = z % 2, 1 - z % 2
+
+    def at(ref, zs, xs, rows):
+        return ref.at[zs // 2, zs % 2, xs, rows]
+
     loads = [
-        pltpu.make_async_copy(part.at[:, at], own, local_sem.at[i])
-        for i, (at, own) in enumerate(((xr, own_r), (xl, own_l), (x, own_m)))
+        pltpu.make_async_copy(part.at[:, :, xs], own.at[i], own_sem.at[i])
+        for i, xs in enumerate((xo, xr, xl, x))
     ]
     for load in loads:
         load.start()
+    own_o, own_r, own_l, own_m = (own.at[i] for i in range(4))
     greet((to_xr, to_xl, to_zr, to_zl))
     mail = Mail(send_sem, recv_sem)
 
-    def half(p, k):
-        return pl.ds(p * n + k * h, h)
-
-    def x12(p):
-        a, b = half(p, 0), half(p, 1)
-        mail.send(("x1r", p), part.at[:, xo, a], x1_l.at[p], to_xr)
-        mail.send(("x1l", p), part.at[:, xo, b], x1_r.at[p], to_xl)
-        mail.send(("x2r", p), part.at[:, xr, b], x2_l.at[p], to_xr)
-        mail.send(("x2l", p), part.at[:, xl, a], x2_r.at[p], to_xl)
-
-    def x3(p):
-        a, b = half(p, 0), half(p, 1)
+    def rows(p):
+        return pl.ds(p * n, n), pl.ds(p * n, h), pl.ds(p * n + h, h)
+
+    def r1(p):
+        n_, a, b = rows(p)
+        mail.send(("r1r", p), at(part, zr, xo, n_), r1_l.at[p], to_zr)
+        mail.send(("r1l", p), at(part, zl, xo, n_), r1_r.at[p], to_zl)
+        mail.send(("r2or", p), at(part, zo, xo, a), r2o_l.at[p], to_xr)
+        mail.send(("r2ol", p), at(part, zo, xo, b), r2o_r.at[p], to_xl)
+        mail.send(("r3mr", p), part.at[:, other, xr, n_], r3m_l.at[p], to_xr)
+        mail.send(("r3ml", p), part.at[:, other, xl, n_], r3m_r.at[p], to_xl)
+        mail.send(("r3br", p), part.at[:, same, xr, b], r3b_l.at[p], to_xr)
+        mail.send(("r3al", p), part.at[:, same, xl, a], r3a_r.at[p], to_xl)
+
+    def r2(p):
+        n_, a, b = rows(p)
         if p == 0:
             loads[0].wait()
+        mail.await_recv(("r1r", p), ("r1l", p))
+        add_rows(cz.at[p], (own_o.at[z // 2, same, n_], r1_l.at[p], r1_r.at[p]))
+        mail.send(("r2r", p), cz.at[p, pl.ds(0, h)], r2_l.at[p], to_xr)
+        mail.send(("r2l", p), cz.at[p, pl.ds(h, h)], r2_r.at[p], to_xl)
+
+    def r3(p):
+        n_, a, b = rows(p)
+        if p == 0:
             loads[1].wait()
-        mail.await_recv(("x1r", p))
-        for k in range(4):
-            add_rows(xc_r.at[p, k], (x1_l.at[p, k], own_r.at[k, a]))
-        mail.send(("x3r", p), xc_r.at[p], x3_l.at[p], to_xr)
-        mail.await_recv(("x1l", p))
-        for k in range(4):
-            add_rows(xc_l.at[p, k], (x1_r.at[p, k], own_l.at[k, b]))
-        mail.send(("x3l", p), xc_l.at[p], x3_r.at[p], to_xl)
-
-    def x4(p):
-        a, b = half(p, 0), half(p, 1)
+            loads[2].wait()
+        mail.await_recv(("r2r", p), ("r2or", p))
+        add_rows(cx_r.at[p, z // 2], (own_r.at[z // 2, same, a], r2_l.at[p]))
+        add_rows(cx_r.at[p, zo // 2], (own_r.at[zo // 2, same, a], r2o_l.at[p]))
+        mail.send(("r3ar", p), cx_r.at[p], r3a_l.at[p], to_xr)
+        mail.await_recv(("r2l", p), ("r2ol", p))
+        add_rows(cx_l.at[p, z // 2], (own_l.at[z // 2, same, b], r2_r.at[p]))
+        add_rows(cx_l.at[p, zo // 2], (own_l.at[zo // 2, same, b], r2o_r.at[p]))
+        mail.send(("r3bl", p), cx_l.at[p], r3b_r.at[p], to_xl)
+
+    def r4(p):
+        n_, a, b = rows(p)
+        first, second = pl.ds(0, h), pl.ds(h, h)
         if p == 0:
-            loads[2].wait()
-        mail.await_recv(("x2l", p), ("x3r", p))
-        for k in range(4):
-            add_rows(sx.at[p, 0, k], (own_m.at[k, a], x3_l.at[p, k], x2_r.at[p, k]))
-        mail.send(("z1r", p), sx.at[p, 0, zo], z1_l.at[p], to_zr)
-        mail.send(("z2l", p), sx.at[p, 0, zl], z2_r.at[p], to_zl)
-        mail.await_recv(("x2r", p), ("x3l", p))
-        for k in range(4):
-            add_rows(sx.at[p, 1, k], (own_m.at[k, b], x3_r.at[p, k], x2_l.at[p, k]))
-        mail.send(("z1l", p), sx.at[p, 1, zo], z1_r.at[p], to_zl)
-        mail.send(("z2r", p), sx.at[p, 1, zr], z2_l.at[p], to_zr)
-
-    def z3(p):
-        mail.await_recv(("z1r", p))
-        add_rows(zc_r.at[p], (z1_l.at[p], sx.at[p, 0, zr]))
-        mail.send(("z3r", p), zc_r.at[p], z3_l.at[p], to_zr)
-        mail.await_recv(("z1l", p))
-        add_rows(zc_l.at[p], (z1_r.at[p], sx.at[p, 1, zl]))
-        mail.send(("z3l", p), zc_l.at[p], z3_r.at[p], to_zl)
-
-    def z4(p):
-        a, b = half(p, 0), half(p, 1)
-        mail.await_recv(("z2l", p), ("z3r", p))
-        dense_relu(hid.at[a], (sx.at[p, 0, z], z3_l.at[p], z2_r.at[p]), weight)
-        mail.await_recv(("z2r", p), ("z3l", p))
-        dense_relu(hid.at[b], (sx.at[p, 1, z], z3_r.at[p], z2_l.at[p]), weight)
-        mail.send(("g1ar", p), hid.at[a], out.at[z, x, a], to_zr)
-        mail.send(("g1bl", p), hid.at[b], out.at[z, x, b], to_zl)
-        mail.send(("g1br", p), hid.at[b], out.at[z, x, b], to_zr)
-        mail.send(("g1al", p), hid.at[a], out.at[z, x, a], to_zl)
-        whole = pl.ds(p * n, n)
-        pltpu.make_async_copy(hid.at[whole], out.at[z, x, whole], hid_sem.at[p]).start()
+            loads[3].wait()
+        mail.await_recv(("r3ar", p), ("r3al", p))
+        for k in range(2):
+            add_rows(sx.at[p, k, same, first], (own_m.at[k, same, a], r3a_l.at[p, k], r3a_r.at[p, k]))
+        mail.send(("r4r", p), sx.at[p, zo // 2, same, first], r4_l.at[p], to_zr)
+        mail.await_recv(("r3br", p), ("r3bl", p))
+        for k in range(2):
+            add_rows(sx.at[p, k, same, second], (own_m.at[k, same, b], r3b_l.at[p, k], r3b_r.at[p, k]))
+        mail.send(("r4l", p), sx.at[p, zo // 2, same, second], r4_r.at[p], to_zl)
+        mail.await_recv(("r3mr", p), ("r3ml", p))
+        for k in range(2):
+            add_rows(sx.at[p, k, other], (own_m.at[k, other, n_], r3m_l.at[p, k], r3m_r.at[p, k]))
+        mail.send(("r5br", p), sx.at[p, zr // 2, other, second], r5b_l.at[p], to_zr)
+        mail.send(("r5al", p), sx.at[p, zl // 2, other, first], r5a_r.at[p], to_zl)
+
+    def r5(p):
+        mail.await_recv(("r4r", p))
+        add_rows(cs_r.at[p], (sx.at[p, zr // 2, other, pl.ds(0, h)], r4_l.at[p]))
+        mail.send(("r5ar", p), cs_r.at[p], r5a_l.at[p], to_zr)
+        mail.await_recv(("r4l", p))
+        add_rows(cs_l.at[p], (sx.at[p, zl // 2, other, pl.ds(h, h)], r4_r.at[p]))
+        mail.send(("r5bl", p), cs_l.at[p], r5b_r.at[p], to_zl)
+
+    def dense(p):
+        n_, a, b = rows(p)
+        mine = sx.at[p, z // 2, same]
+        mail.await_recv(("r5ar", p), ("r5al", p))
+        dense_relu(hid.at[a], (mine.at[pl.ds(0, h)], r5a_l.at[p], r5a_r.at[p]), weight)
+        mail.send(("g1ar", p), hid.at[a], at(out, z, x, a), to_zr)
+        mail.send(("g3ar", p), hid.at[a], at(out, z, x, a), to_xr)
+        mail.await_recv(("r5br", p), ("r5bl", p))
+        dense_relu(hid.at[b], (mine.at[pl.ds(h, h)], r5b_l.at[p], r5b_r.at[p]), weight)
+        mail.send(("g1bl", p), hid.at[b], at(out, z, x, b), to_zl)
+        mail.send(("g3bl", p), hid.at[b], at(out, z, x, b), to_xl)
+        mail.send(("g1br", p), hid.at[b], at(out, z, x, b), to_zr)
+        mail.send(("g1al", p), hid.at[a], at(out, z, x, a), to_zl)
+        mail.send(("g3br", p), hid.at[b], at(out, z, x, b), to_xr)
+        mail.send(("g3al", p), hid.at[a], at(out, z, x, a), to_xl)
+        pltpu.make_async_copy(hid.at[n_], at(out, z, x, n_), hid_sem.at[p]).start()
+
+    def pass_on(name, p, zs, xs, rows_, to):
+        mail.send((name, p), at(out, zs, xs, rows_), at(out, zs, xs, rows_), to)
 
     def g2(p):
-        a, b = half(p, 0), half(p, 1)
+        n_, a, b = rows(p)
         mail.await_recv(("g1ar", p))
-        mail.send(("g2r", p), out.at[zl, x, a], out.at[zl, x, a], to_zr)
+        pass_on("g2r", p, zl, x, a, to_zr)
         mail.await_recv(("g1bl", p))
-        mail.send(("g2l", p), out.at[zr, x, b], out.at[zr, x, b], to_zl)
+        pass_on("g2l", p, zr, x, b, to_zl)
+
+    def g4(p):
+        n_, a, b = rows(p)
+        mail.await_recv(("g3ar", p))
+        pass_on("g4r", p, z, xl, a, to_xr)
+        mail.await_recv(("g3bl", p))
+        pass_on("g4l", p, z, xr, b, to_xl)
+
+    def g5(p):
+        n_, a, b = rows(p)
+        mail.await_recv(("g4r", p), ("g4l", p))
+        pass_on("g5r", p, z, xo, n_, to_zr)
+        pass_on("g5l", p, z, xo, n_, to_zl)
 
     def g3(p):
-        a, b = half(p, 0), half(p, 1)
-        mail.await_recv(("g1br", p), ("g1al", p), ("g2r", p), ("g2l", p))
-        whole = pl.ds(p * n, n)
-        pltpu.make_async_copy(hid.at[whole], out.at[z, x, whole], hid_sem.at[p]).wait()
-        for name, rows, to in (("g3ar", a, to_xr), ("g3bl", b, to_xl), ("g3br", b, to_xr), ("g3al", a, to_xl)):
-            mail.send((name, p), out.at[:, x, rows], out.at[:, x, rows], to)
-
-    def g4(p):
-        a, b = half(p, 0), half(p, 1)
-        mail.await_recv(("g3ar", p))
-        mail.send(("g4r", p), out.at[:, xl, a], out.at[:, xl, a], to_xr)
-        mail.await_recv(("g3bl", p))
-        mail.send(("g4l", p), out.at[:, xr, b], out.at[:, xr, b], to_xl)
-
-    def g5(p):
-        mail.await_recv(("g3br", p), ("g3al", p), ("g4r", p), ("g4l", p))
-
-    stages = ((x12, 0), (x3, 1), (x4, 2), (z3, 3), (z4, 4), (g2, 5), (g3, 6), (g4, 7), (g5, 8))
-    for tick in range(PARTS + len(stages) - 1):
-        for stage, lag in stages:
-            if 0 <= tick - lag < PARTS:
-                stage(tick - lag)
+        n_, a, b = rows(p)
+        mail.await_recv(("g1br", p), ("g1al", p))
+        both = out.at[:, other, x, n_]
+        mail.send(("g3mr", p), both, both, to_xr)
+        mail.send(("g3ml", p), both, both, to_xl)
+
+    def g3o(p):
+        n_, a, b = rows(p)
+        mail.await_recv(("g2r", p))
+        pass_on("g3oar", p, zo, x, a, to_xr)
+        mail.await_recv(("g2l", p))
+        pass_on("g3obl", p, zo, x, b, to_xl)
+        pass_on("g3obr", p, zo, x, b, to_xr)
+        pass_on("g3oal", p, zo, x, a, to_xl)
+
+    def g4o(p):
+        n_, a, b = rows(p)
+        mail.await_recv(("g3oar", p))
+        pass_on("g4or", p, zo, xl, a, to_xr)
+        mail.await_recv(("g3obl", p))
+        pass_on("g4ol", p, zo, xr, b, to_xl)
+
+    def end(p):
+        n_, a, b = rows(p)
+        pltpu.make_async_copy(hid.at[n_], at(out, z, x, n_), hid_sem.at[p]).wait()
+        mail.await_recv(*((name, p) for name in (
+            "g3br", "g3al", "g3mr", "g3ml", "g3obr", "g3oal", "g4or", "g4ol", "g5r", "g5l"
+        )))
+
+    stages = dict(
+        r1=r1, r2=r2, r3=r3, r4=r4, r5=r5, d=dense, g2=g2, g4=g4, g5=g5, g3=g3, g3o=g3o, g4o=g4o,
+        end=end,
+    )
+    order = sorted(stages, key=lambda name: -LAGS[name])
+    for tick in range(PARTS + max(LAGS.values())):
+        for name in order:
+            if 0 <= tick - LAGS[name] < PARTS:
+                stages[name](tick - LAGS[name])
     mail.finish()
 
 
 def row_exchange(part, weight):
     _, slab, width = part.shape
-    h = slab // PARTS // 2
+    n = slab // PARTS
+    h = n // 2
     dt = part.dtype
     hbm = pl.BlockSpec(memory_space=pl.ANY)
-    count = 24 * PARTS
+    count = 40 * PARTS
+
+    def buf(*lead):
+        return [pltpu.VMEM((PARTS, *lead, width), dt)]
+
     out = pl.pallas_call(
         row_kernel,
-        out_shape=jax.ShapeDtypeStruct((4, 4, slab, width), dt),
+        out_shape=jax.ShapeDtypeStruct((2, 2, 4, slab, width), dt),
         in_specs=[hbm, pl.BlockSpec(memory_space=pltpu.VMEM)],
         out_specs=hbm,
         scratch_shapes=(
-            [pltpu.VMEM((4, slab, width), dt)] * 3
-            + [pltpu.VMEM((PARTS, 4, h, width), dt)] * 8
-            + [pltpu.VMEM((PARTS, 2, 4, h, width), dt)]
-            + [pltpu.VMEM((PARTS, h, width), dt)] * 8
+            [pltpu.VMEM((4, 2, 2, slab, width), dt)]
+            + buf(n) * 3 + buf(h) * 4 + buf(2, h) * 2 + buf(2, n) * 2 + buf(2, h) * 4
+            + buf(2, 2, n) + buf(h) * 8
             + [pltpu.VMEM((slab, width), dt)]
             + [pltpu.SemaphoreType.DMA((count,))] * 2
-            + [pltpu.SemaphoreType.DMA((3,)), pltpu.SemaphoreType.DMA((PARTS,))]
+            + [pltpu.SemaphoreType.DMA((4,)), pltpu.SemaphoreType.DMA((PARTS,))]
         ),
         compiler_params=pltpu.CompilerParams(
             collective_id=1, has_side_effects=True, vmem_limit_bytes=60 << 20
         ),
-    )(part.reshape(4, 4, slab, width), weight)
+    )(part.reshape(2, 2, 4, slab, width), weight)
     return out.reshape(16, slab, width)
 
 

time: 244 us -> 217 us (0.89)
  Pallas kernels: 240 us -> 214 us
    pallas_call x1, Pallas kernels: 152 us -> 115 us  [row_exchange(): pl.pallas_call(row_kernel, out_shape=jax.ShapeDtypeStruct((2, 2, 4, slab,...]
    pallas_call x1, Pallas kernels: 38.3 us -> 48.4 us  [col_sum(): pl.pallas_call(sum_kernel, out_shape=jax.ShapeDtypeStruct((slab, width),...]
where the time goes in v3:
time: 217 us; the launch traced here: 216 us
  Pallas kernels  214 us (99%)
    pallas_call x1, Pallas kernels, row_exchange(): pl.pallas_call(row_kernel, out_shape=jax.ShapeDtypeStruct((2, 2, 4, slab,...  115 us
    pallas_call x1, Pallas kernels, col_sum(): pl.pallas_call(sum_kernel, out_shape=jax.ShapeDtypeStruct((slab, width),...  48.4 us
    pallas_call x1, Pallas kernels, col_gather(): pl.pallas_call(gather_kernel, out_shape=jax.ShapeDtypeStruct((2, 4, 2, sl...  33.1 us
    pallas_call x2, Pallas kernels, block_product(): pl.pallas_call(functools.partial(product_kernel, transposed, unroll), out...  17.2 us

profile of v3, /device:TPU:1, one launch (start us, length us, event | category | flops | bytes accessed | tf_op | source)
XLA Modules:
  0.0 216.4 jit_solution(450165195028870547)
XLA Ops:
  0.7 33.1 %shard_map.82 = bf16[2,4,2,768,256]{4,3,2,1,0:T(8,128)(2,1)} custom-call(s32[1,768]{1,0:T(1,128)} %order.1, bf16[768,256]{1,0:T(8,128)(2,1)} %features.1), custom_call_target="tpu_custom_call" | custom-call | tf_op jit(solution)/shard_map/pallas_call | solution.py:348
  33.7 8.7 %shard_map.83 = bf16[96,128,256]{2,1,0:T(8,128)(2,1)} custom-call(s32[1,192]{1,0:T(1,128)} %bitcast.15, s32[1,192]{1,0:T(1,128)} %bitcast.13, s32[1,1]{1,0:T(1,128)S(6)} %copy.10.count_ref, bf16[96,128,256]{2,1,0:T(8,128)(2,1)} %bitcast.12, bf16[192,128,128]{2,1,0:T(8,128)(2,1)} %bitcast.9), custom_call_target="tpu_custom_call" | custom-call | flops 1610612736 | bytes 18874368 | tf_op jit(solution)/shard_map/pallas_call | solution.py:520
  42.4 115.3 %shard_map.84 = bf16[2,2,4,768,256]{4,3,2,1,0:T(8,128)(2,1)} custom-call(bf16[2,2,4,768,256]{4,3,2,1,0:T(8,128)(2,1)} %bitcast.8, bf16[256,256]{1,0:T(8,128)(2,1)} %weight.2), custom_call_target="tpu_custom_call" | custom-call | tf_op jit(solution)/shard_map/pallas_call | solution.py:250
  157.8 8.5 %shard_map.85 = bf16[96,128,256]{2,1,0:T(8,128)(2,1)} custom-call(s32[1,192]{1,0:T(1,128)} %bitcast.14, s32[1,192]{1,0:T(1,128)} %bitcast.16, s32[1,1]{1,0:T(1,128)S(6)} %copy.10.count_ref, bf16[96,128,256]{2,1,0:T(8,128)(2,1)} %bitcast.7, bf16[192,128,128]{2,1,0:T(8,128)(2,1)} %bitcast.10), custom_call_target="tpu_custom_call" | custom-call | flops 1610612736 | bytes 18874368 | tf_op jit(solution)/shard_map/pallas_call | solution.py:520
  166.3 48.4 %shard_map.86 = bf16[768,256]{1,0:T(8,128)(2,1)} custom-call(bf16[2,4,2,768,256]{4,3,2,1,0:T(8,128)(2,1)} %bitcast.11, bf16[256,256]{1,0:T(8,128)(2,1)} %weight.3), custom_call_target="tpu_custom_call" | custom-call | tf_op jit(solution)/shard_map/pallas_call | solution.py:433
  214.7 1.8 copy.11

commit v4 on v3

--- a/solution.py
+++ b/solution.py
@@ -62,9 +62,9 @@
 
 
 def row_kernel(
-    part, weight, out, own, r1_l, r1_r, cz, r2_l, r2_r, r2o_l, r2o_r, cx_r, cx_l, r3m_l, r3m_r,
+    part, weight, out, r1_l, r1_r, cz, r2_l, r2_r, r2o_l, r2o_r, cx_r, cx_l, r3m_l, r3m_r,
     r3b_l, r3a_r, r3a_l, r3b_r, sx, r4_l, r4_r, r5b_l, r5a_r, r5a_l, r5b_r, cs_r, cs_l, hid,
-    send_sem, recv_sem, own_sem, hid_sem,
+    send_sem, recv_sem, hid_sem,
 ):
     slab = part.shape[3]
     n = slab // PARTS
@@ -80,13 +80,6 @@
     def at(ref, zs, xs, rows):
         return ref.at[zs // 2, zs % 2, xs, rows]
 
-    loads = [
-        pltpu.make_async_copy(part.at[:, :, xs], own.at[i], own_sem.at[i])
-        for i, xs in enumerate((xo, xr, xl, x))
-    ]
-    for load in loads:
-        load.start()
-    own_o, own_r, own_l, own_m = (own.at[i] for i in range(4))
     greet((to_xr, to_xl, to_zr, to_zl))
     mail = Mail(send_sem, recv_sem)
 
@@ -106,43 +99,36 @@
 
     def r2(p):
         n_, a, b = rows(p)
-        if p == 0:
-            loads[0].wait()
         mail.await_recv(("r1r", p), ("r1l", p))
-        add_rows(cz.at[p], (own_o.at[z // 2, same, n_], r1_l.at[p], r1_r.at[p]))
+        add_rows(cz.at[p], (part.at[z // 2, same, xo, n_], r1_l.at[p], r1_r.at[p]))
         mail.send(("r2r", p), cz.at[p, pl.ds(0, h)], r2_l.at[p], to_xr)
         mail.send(("r2l", p), cz.at[p, pl.ds(h, h)], r2_r.at[p], to_xl)
 
     def r3(p):
         n_, a, b = rows(p)
-        if p == 0:
-            loads[1].wait()
-            loads[2].wait()
         mail.await_recv(("r2r", p), ("r2or", p))
-        add_rows(cx_r.at[p, z // 2], (own_r.at[z // 2, same, a], r2_l.at[p]))
-        add_rows(cx_r.at[p, zo // 2], (own_r.at[zo // 2, same, a], r2o_l.at[p]))
+        add_rows(cx_r.at[p, z // 2], (part.at[z // 2, same, xr, a], r2_l.at[p]))
+        add_rows(cx_r.at[p, zo // 2], (part.at[zo // 2, same, xr, a], r2o_l.at[p]))
         mail.send(("r3ar", p), cx_r.at[p], r3a_l.at[p], to_xr)
         mail.await_recv(("r2l", p), ("r2ol", p))
-        add_rows(cx_l.at[p, z // 2], (own_l.at[z // 2, same, b], r2_r.at[p]))
-        add_rows(cx_l.at[p, zo // 2], (own_l.at[zo // 2, same, b], r2o_r.at[p]))
+        add_rows(cx_l.at[p, z // 2], (part.at[z // 2, same, xl, b], r2_r.at[p]))
+        add_rows(cx_l.at[p, zo // 2], (part.at[zo // 2, same, xl, b], r2o_r.at[p]))
         mail.send(("r3bl", p), cx_l.at[p], r3b_r.at[p], to_xl)
 
     def r4(p):
         n_, a, b = rows(p)
         first, second = pl.ds(0, h), pl.ds(h, h)
-        if p == 0:
-            loads[3].wait()
         mail.await_recv(("r3ar", p), ("r3al", p))
         for k in range(2):
-            add_rows(sx.at[p, k, same, first], (own_m.at[k, same, a], r3a_l.at[p, k], r3a_r.at[p, k]))
+            add_rows(sx.at[p, k, same, first], (part.at[k, same, x, a], r3a_l.at[p, k], r3a_r.at[p, k]))
         mail.send(("r4r", p), sx.at[p, zo // 2, same, first], r4_l.at[p], to_zr)
         mail.await_recv(("r3br", p), ("r3bl", p))
         for k in range(2):
-            add_rows(sx.at[p, k, same, second], (own_m.at[k, same, b], r3b_l.at[p, k], r3b_r.at[p, k]))
+            add_rows(sx.at[p, k, same, second], (part.at[k, same, x, b], r3b_l.at[p, k], r3b_r.at[p, k]))
         mail.send(("r4l", p), sx.at[p, zo // 2, same, second], r4_r.at[p], to_zl)
         mail.await_recv(("r3mr", p), ("r3ml", p))
         for k in range(2):
-            add_rows(sx.at[p, k, other], (own_m.at[k, other, n_], r3m_l.at[p, k], r3m_r.at[p, k]))
+            add_rows(sx.at[p, k, other], (part.at[k, other, x, n_], r3m_l.at[p, k], r3m_r.at[p, k]))
         mail.send(("r5br", p), sx.at[p, zr // 2, other, second], r5b_l.at[p], to_zr)
         mail.send(("r5al", p), sx.at[p, zl // 2, other, first], r5a_r.at[p], to_zl)
 
@@ -241,7 +227,7 @@
     n = slab // PARTS
     h = n // 2
     dt = part.dtype
-    hbm = pl.BlockSpec(memory_space=pl.ANY)
+    vmem = pl.BlockSpec(memory_space=pltpu.VMEM)
     count = 40 * PARTS
 
     def buf(*lead):
@@ -250,18 +236,17 @@
     out = pl.pallas_call(
         row_kernel,
         out_shape=jax.ShapeDtypeStruct((2, 2, 4, slab, width), dt),
-        in_specs=[hbm, pl.BlockSpec(memory_space=pltpu.VMEM)],
-        out_specs=hbm,
+        in_specs=[vmem, vmem],
+        out_specs=vmem,
         scratch_shapes=(
-            [pltpu.VMEM((4, 2, 2, slab, width), dt)]
-            + buf(n) * 3 + buf(h) * 4 + buf(2, h) * 2 + buf(2, n) * 2 + buf(2, h) * 4
+            buf(n) * 3 + buf(h) * 4 + buf(2, h) * 2 + buf(2, n) * 2 + buf(2, h) * 4
             + buf(2, 2, n) + buf(h) * 8
             + [pltpu.VMEM((slab, width), dt)]
             + [pltpu.SemaphoreType.DMA((count,))] * 2
-            + [pltpu.SemaphoreType.DMA((4,)), pltpu.SemaphoreType.DMA((PARTS,))]
+            + [pltpu.SemaphoreType.DMA((PARTS,))]
         ),
         compiler_params=pltpu.CompilerParams(
-            collective_id=1, has_side_effects=True, vmem_limit_bytes=60 << 20
+            collective_id=1, has_side_effects=True, vmem_limit_bytes=28 << 20
         ),
     )(part.reshape(2, 2, 4, slab, width), weight)
     return out.reshape(16, slab, width)
@@ -269,76 +254,88 @@
 
 def gather_kernel(order, features, out, own, send_sem, recv_sem, own_sem):
     slab = features.shape[0]
-    h = slab // 2
+    h = slab // 4
     me = lax.axis_index("col")
     zp, y, c = me // 8, (me // 2) % 4, me % 2
     yr, yl, yo, zq = (y + 1) % 4, (y + 3) % 4, (y + 2) % 4, 1 - zp
     to_r, to_l = {"col": zp * 8 + yr * 2 + c}, {"col": zp * 8 + yl * 2 + c}
     to_z, to_c = {"col": zq * 8 + y * 2 + c}, {"col": zp * 8 + y * 2 + 1 - c}
-    step = 128 if h % 128 == 0 else h
-
-    def place(half):
-        @pl.loop(0, h // step)
-        def _(i):
-            at = pl.ds(pl.multiple_of(half * h + i * step, step), step)
-            place_of = order[:, at]
-            chosen = lax.broadcasted_iota(jnp.int32, (slab, step), 0) == place_of
-            own[at] = lax.dot_general(
-                chosen.astype(features.dtype), features[...], (((0,), (0,)), ((), ())),
-                preferred_element_type=jnp.float32,
-            ).astype(own.dtype)
-
-    place(0)
+
+    def place(q):
+        at = pl.ds(q * h, h)
+        chosen = lax.broadcasted_iota(jnp.int32, (slab, h), 0) == order[:, at]
+        own[at] = lax.dot_general(
+            chosen.astype(features.dtype), features[...], (((0,), (0,)), ((), ())),
+            preferred_element_type=jnp.float32,
+        ).astype(own.dtype)
+
+    for q in (0, 2):
+        place(q)
     greet((to_r, to_l, to_z, to_c))
     mail = Mail(send_sem, recv_sem)
-    a, b, whole = pl.ds(0, h), pl.ds(h, h), pl.ds(0, slab)
-
-    def send_own(name, rows, to):
-        mail.send(name, own.at[rows], out.at[zp, y, c, rows], to)
+    whole, lower, upper = pl.ds(0, slab), pl.ds(0, 2 * h), pl.ds(2 * h, 2 * h)
+
+    def send_own(name, q, to):
+        rows = pl.ds(q * h, h)
+        mail.send((name, q), own.at[rows], out.at[zp, y, c, rows], to)
 
     def send_on(name, zs, ys, rows, to):
         mail.send(name, out.at[zs, ys, c, rows], out.at[zs, ys, c, rows], to)
 
-    send_own("ar", a, to_r)
-    send_own("za", a, to_z)
-    place(1)
-    send_own("bl", b, to_l)
-    send_own("zb", b, to_z)
-    send_own("br", b, to_r)
-    send_own("al", a, to_l)
-    send_own("c0", whole, to_c)
+    def quarter(q):
+        return pl.ds(q * h, h)
+
+    for q in (0, 2):
+        send_own("r" if q == 0 else "l", q, to_r if q == 0 else to_l)
+        send_own("z", q, to_z)
+    for q in (1, 3):
+        place(q)
+        send_own("r" if q == 1 else "l", q, to_r if q == 1 else to_l)
+        send_own("z", q, to_z)
+    send_own("r", 2, to_r)
+    send_own("l", 0, to_l)
+    mail.send("c0", own, out.at[zp, y, c], to_c)
     own_copy = pltpu.make_async_copy(own, out.at[zp, y, c], own_sem)
     own_copy.start()
-    mail.await_recv("ar")
-    send_on("fr", zp, yl, a, to_r)
-    mail.await_recv("bl")
-    send_on("fl", zp, yr, b, to_l)
-    mail.await_recv("za")
-    send_on("par", zq, y, a, to_r)
-    send_on("pal", zq, y, a, to_l)
-    mail.await_recv("zb")
-    send_on("pbr", zq, y, b, to_r)
-    send_on("pbl", zq, y, b, to_l)
+    mail.await_recv(("r", 0))
+    send_on(("fr", 0), zp, yl, quarter(0), to_r)
+    mail.await_recv(("l", 2))
+    send_on(("fl", 2), zp, yr, quarter(2), to_l)
+    send_own("r", 3, to_r)
+    send_own("l", 1, to_l)
+    mail.await_recv(("r", 1))
+    send_on(("fr", 1), zp, yl, quarter(1), to_r)
+    mail.await_recv(("l", 3))
+    send_on(("fl", 3), zp, yr, quarter(3), to_l)
+    for q in (0, 2):
+        mail.await_recv(("z", q))
+        send_on(("pr", q), zq, y, quarter(q), to_r)
+        send_on(("pl", q), zq, y, quarter(q), to_l)
+    mail.await_recv(("fr", 0))
+    send_on(("zo", 0), zp, yo, quarter(0), to_z)
+    mail.await_recv(("fl", 2))
+    send_on(("zo", 2), zp, yo, quarter(2), to_z)
+    for q in (1, 3):
+        mail.await_recv(("z", q))
+        send_on(("pr", q), zq, y, quarter(q), to_r)
+        send_on(("pl", q), zq, y, quarter(q), to_l)
     send_on("c1", zq, y, whole, to_c)
-    mail.await_recv("br")
+    mail.await_recv(("r", 2), ("r", 3), ("l", 0), ("l", 1))
     send_on("c2", zp, yl, whole, to_c)
-    mail.await_recv("al")
     send_on("c3", zp, yr, whole, to_c)
-    mail.await_recv("fr")
-    send_on("zoa", zp, yo, a, to_z)
-    mail.await_recv("fl")
-    send_on("zob", zp, yo, b, to_z)
+    mail.await_recv(("fr", 1))
+    send_on(("zo", 1), zp, yo, quarter(1), to_z)
+    mail.await_recv(("fl", 3))
+    send_on(("zo", 3), zp, yo, quarter(3), to_z)
     send_on("c4", zp, yo, whole, to_c)
-    mail.await_recv("par", "pbr")
-    send_on("c5", zq, yl, whole, to_c)
-    mail.await_recv("pal", "pbl")
-    send_on("c6", zq, yr, whole, to_c)
-    mail.await_recv("zoa")
-    send_on("c7a", zq, yo, a, to_c)
-    mail.await_recv("zob")
-    send_on("c7b", zq, yo, b, to_c)
+    last = []
+    for q in (0, 2, 1, 3):
+        for name, zs, ys in (("pr", zq, yl), ("pl", zq, yr), ("zo", zq, yo)):
+            mail.await_recv((name, q))
+            last.append(("c" + name, q))
+            send_on(last[-1], zs, ys, quarter(q), to_c)
     own_copy.wait()
-    mail.await_recv("c0", "c1", "c2", "c3", "c4", "c5", "c6", "c7a", "c7b")
+    mail.await_recv("c0", "c1", "c2", "c3", "c4", *last)
     mail.finish()
 
 
@@ -349,23 +346,23 @@
         gather_kernel,
         out_shape=jax.ShapeDtypeStruct((2, 4, 2, slab, width), features.dtype),
         in_specs=[vmem, vmem],
-        out_specs=pl.BlockSpec(memory_space=pl.ANY),
+        out_specs=vmem,
         scratch_shapes=[
             pltpu.VMEM((slab, width), features.dtype),
-            pltpu.SemaphoreType.DMA((23,)),
-            pltpu.SemaphoreType.DMA((23,)),
+            pltpu.SemaphoreType.DMA((45,)),
+            pltpu.SemaphoreType.DMA((45,)),
             pltpu.SemaphoreType.DMA,
         ],
         compiler_params=pltpu.CompilerParams(
-            collective_id=0, has_side_effects=True, vmem_limit_bytes=60 << 20
+            collective_id=0, has_side_effects=True, vmem_limit_bytes=16 << 20
         ),
     )(order, features)
     return out.reshape(16, slab, width)
 
 
 def sum_kernel(
-    part, weight, out, own, sib, both, z1, s2_l, s2_r, s3_l, s3_r, opp, s4b_l, s4b_r, s4a_l, s4a_r,
-    c_r, c_l, via, z2, send_sem, recv_sem, own_sem,
+    part, weight, out, sib, both, z1, s2_l, s2_r, s3_l, s3_r, opp, s4b_l, s4b_r, s4a_l, s4a_r,
+    c_r, c_l, via, z2, send_sem, recv_sem,
 ):
     slab = part.shape[3]
     h = slab // 2
@@ -376,21 +373,15 @@
     to_z, to_c = {"col": zq * 8 + y * 2 + c}, {"col": zp * 8 + y * 2 + d}
     a, b = pl.ds(0, h), pl.ds(h, h)
     dests = ((zq, yo), (zq, yr), (zq, yl), (zp, yr), (zp, yl), (zp, yo), (zq, y), (zp, y))
-    loads = [
-        pltpu.make_async_copy(part.at[zs, ys, c], own.at[i], own_sem.at[i])
-        for i, (zs, ys) in enumerate(dests)
-    ]
-    for load in loads:
-        load.start()
     greet((to_r, to_l, to_z, to_c))
     mail = Mail(send_sem, recv_sem)
     for i, (zs, ys) in enumerate(dests):
         mail.send(("c", i), part.at[zs, ys, d], sib.at[i], to_c)
 
     def join(i):
-        loads[i].wait()
+        zs, ys = dests[i]
         mail.await_recv(("c", i))
-        add_rows(both.at[i], (own.at[i], sib.at[i]))
+        add_rows(both.at[i], (part.at[zs, ys, c], sib.at[i]))
 
     join(0)
     mail.send("z1", both.at[0], z1, to_z)
@@ -433,16 +424,15 @@
     return pl.pallas_call(
         sum_kernel,
         out_shape=jax.ShapeDtypeStruct((slab, width), dt),
-        in_specs=[pl.BlockSpec(memory_space=pl.ANY), vmem],
+        in_specs=[vmem, vmem],
         out_specs=vmem,
         scratch_shapes=(
-            [pltpu.VMEM((8, slab, width), dt)] * 3
+            [pltpu.VMEM((8, slab, width), dt)] * 2
             + [full] * 3 + [half] * 2 + [full] + [half] * 6 + [full] * 2
             + [pltpu.SemaphoreType.DMA((18,))] * 2
-            + [pltpu.SemaphoreType.DMA((8,))]
         ),
         compiler_params=pltpu.CompilerParams(
-            collective_id=2, has_side_effects=True, vmem_limit_bytes=60 << 20
+            collective_id=2, has_side_effects=True, vmem_limit_bytes=28 << 20
         ),
     )(part.reshape(2, 4, 2, slab, width), weight)
 
@@ -451,11 +441,11 @@
 
 
 def product_kernel(
-    transposed, unroll, source_ref, target_ref, count_ref, panel_hbm, tile_hbm, out_hbm,
-    tiles, panel, total, tile_sem, panel_sem, out_sem,
+    transposed, unroll, source_ref, target_ref, count_ref, panel, tile_hbm, out,
+    tiles, total, tile_sem,
 ):
-    slots, block = tile_hbm.shape[0], tile_hbm.shape[1]
-    blocks = panel_hbm.shape[0]
+    slots = tile_hbm.shape[0]
+    blocks = panel.shape[0]
     chunks = slots // CHUNK
     live = count_ref[0, 0]
 
@@ -463,8 +453,6 @@
         part = pl.ds(c * CHUNK, CHUNK)
         return pltpu.make_async_copy(tile_hbm.at[part], tiles.at[part], tile_sem.at[c])
 
-    panel_copy = pltpu.make_async_copy(panel_hbm, panel, panel_sem)
-    panel_copy.start()
     for c in range(chunks):
         pl.when(c * CHUNK < live)(lambda c=c: tile_copy(c).start())
 
@@ -472,65 +460,54 @@
     def _(g):
         total[g] = jnp.zeros_like(total[g])
 
-    panel_copy.wait()
     dims = (((0,), (0,)), ((), ())) if transposed else (((1,), (0,)), ((), ()))
+
+    def some_slots(first):
+        products, targets = [], []
+        for k in range(unroll):
+            slot = first + k
+            products.append(lax.dot_general(
+                tiles[slot], panel[source_ref[0, slot]], dims, preferred_element_type=jnp.float32
+            ))
+            targets.append(jnp.where(slot < live, target_ref[0, slot], blocks))
+        for k in range(unroll):
+            total[targets[k]] += products[k]
 
     def one_chunk(c):
         tile_copy(c).wait()
-
-        @pl.loop(0, CHUNK // unroll)
-        def _(step):
-            first = c * CHUNK + step * unroll
-
-            @pl.when(first < live)
-            def _():
-                products, targets = [], []
-                for k in range(unroll):
-                    slot = first + k
-                    products.append(lax.dot_general(
-                        tiles[slot], panel[source_ref[0, slot]], dims,
-                        preferred_element_type=jnp.float32,
-                    ))
-                    targets.append(jnp.where(slot < live, target_ref[0, slot], blocks))
-                for k in range(unroll):
-                    total[targets[k]] += products[k]
-
-    for c in range(chunks):
-        pl.when(c * CHUNK < live)(functools.partial(one_chunk, c))
-
-    rounds = 12
-    share = blocks // rounds
-    copies = []
-    for c in range(rounds):
-        @pl.loop(c * share, (c + 1) * share)
-        def _(g):
-            panel[g] = total[g].astype(panel.dtype)
-        part = pl.ds(c * share, share)
-        copies.append(pltpu.make_async_copy(panel.at[part], out_hbm.at[part], out_sem.at[c]))
-        copies[-1].start()
-    for copy in copies:
-        copy.wait()
-
-
-def block_product(panel, tiles, source_ids, target_ids, count, transposed, unroll=8):
+        if unroll == CHUNK:
+            some_slots(c * CHUNK)
+        else:
+            @pl.loop(0, CHUNK // unroll)
+            def _(step):
+                first = c * CHUNK + step * unroll
+                pl.when(first < live)(lambda: some_slots(first))
+
+    @pl.loop(0, chunks)
+    def _(c):
+        pl.when(c * CHUNK < live)(lambda: one_chunk(c))
+
+    @pl.loop(0, blocks)
+    def _(g):
+        out[g] = total[g].astype(out.dtype)
+
+
+def block_product(panel, tiles, source_ids, target_ids, count, transposed, unroll=16):
     slots, block, _ = tiles.shape
     blocks, _, width = panel.shape
     smem = pl.BlockSpec(memory_space=pltpu.SMEM)
-    hbm = pl.BlockSpec(memory_space=pl.ANY)
+    vmem = pl.BlockSpec(memory_space=pltpu.VMEM)
     return pl.pallas_call(
         functools.partial(product_kernel, transposed, unroll),
         out_shape=jax.ShapeDtypeStruct(panel.shape, panel.dtype),
-        in_specs=[smem, smem, smem, hbm, hbm],
-        out_specs=hbm,
+        in_specs=[smem, smem, smem, vmem, pl.BlockSpec(memory_space=pl.ANY)],
+        out_specs=vmem,
         scratch_shapes=[
             pltpu.VMEM(tiles.shape, tiles.dtype),
-            pltpu.VMEM(panel.shape, panel.dtype),
             pltpu.VMEM((blocks + 1, block, width), jnp.float32),
             pltpu.SemaphoreType.DMA((slots // CHUNK,)),
-            pltpu.SemaphoreType.DMA,
-            pltpu.SemaphoreType.DMA((12,)),
         ],
-        compiler_params=pltpu.CompilerParams(vmem_limit_bytes=60 << 20),
+        compiler_params=pltpu.CompilerParams(vmem_limit_bytes=36 << 20),
         cost_estimate=pl.CostEstimate(
             flops=2 * slots * block * block * width, transcendentals=0,
             bytes_accessed=2 * (tiles.size + 2 * panel.size),

time: 217 us -> 191 us (0.88)
  Pallas kernels: 214 us -> 187 us
    pallas_call x1, Pallas kernels: 48.4 us -> 36.8 us  [col_sum(): pl.pallas_call(sum_kernel, out_shape=jax.ShapeDtypeStruct((slab, width),...]
    pallas_call x2, Pallas kernels: 17.2 us -> 7.41 us  [block_product(): pl.pallas_call(functools.partial(product_kernel, transposed, unroll), out...]
    pallas_call x1, Pallas kernels: 115 us -> 112 us  [row_exchange(): pl.pallas_call(row_kernel, out_shape=jax.ShapeDtypeStruct((2, 2, 4, slab,...]
    pallas_call x1, Pallas kernels: 33.1 us -> 30.3 us  [col_gather(): pl.pallas_call(gather_kernel, out_shape=jax.ShapeDtypeStruct((2, 4, 2, sl...]
where the time goes in v4:
time: 191 us; the launch traced here: 190 us
  Pallas kernels  187 us (98%)
  local copies, waits for them, and re-layouts  2.44 us (1%)
    pallas_call x1, Pallas kernels, row_exchange(): pl.pallas_call(row_kernel, out_shape=jax.ShapeDtypeStruct((2, 2, 4, slab,...  112 us
    pallas_call x1, Pallas kernels, col_sum(): pl.pallas_call(sum_kernel, out_shape=jax.ShapeDtypeStruct((slab, width),...  36.8 us
    pallas_call x1, Pallas kernels, col_gather(): pl.pallas_call(gather_kernel, out_shape=jax.ShapeDtypeStruct((2, 4, 2, sl...  30.3 us
    pallas_call x2, Pallas kernels, block_product(): pl.pallas_call(functools.partial(product_kernel, transposed, unroll), out...  7.41 us

profile of v4, /device:TPU:1, one launch (start us, length us, event | category | flops | bytes accessed | tf_op | source)
XLA Modules:
  0.0 190.2 jit_solution(6440152540673044940)
XLA Ops:
  0.0 0.0 copy-start.3
  0.0 0.0 copy-start.4
  0.7 0.0 copy-start
  0.7 1.0 copy-done
  1.7 0.0 copy-start.5
  1.7 0.7 copy-done.5
  2.4 30.3 %shard_map.82 = bf16[2,4,2,768,256]{4,3,2,1,0:T(8,128)(2,1)S(1)} custom-call(s32[1,768]{1,0:T(1,128)S(1)} %copy-done.5, bf16[768,256]{1,0:T(8,128)(2,1)S(1)} %copy-done), custom_call_target="tpu_custom_call" | custom-call | tf_op jit(solution)/shard_map/pallas_call | solution.py:345
  32.7 0.0 copy-done.3
  32.7 0.0 copy-done.4
  32.7 0.0 copy-start.1
  32.7 3.7 %shard_map.83 = bf16[96,128,256]{2,1,0:T(8,128)(2,1)S(1)} custom-call(s32[1,192]{1,0:T(1,128)S(1)} %bitcast.13, s32[1,192]{1,0:T(1,128)S(1)} %bitcast.11, s32[1,1]{1,0:T(1,128)S(6)} %copy.10.count_ref, bf16[96,128,256]{2,1,0:T(8,128)(2,1)S(1)} %bitcast.10, bf16[192,128,128]{2,1,0:T(8,128)(2,1)} %bitcast.15), custom_call_target="tpu_custom_call" | custom-call | flops 1610612736 | bytes 18874368 | tf_op jit(solution)/shard_map/pallas_call | solution.py:500
  36.5 0.0 copy-done.1
  36.5 112.5 %shard_map.84 = bf16[2,2,4,768,256]{4,3,2,1,0:T(8,128)(2,1)S(1)} custom-call(bf16[2,2,4,768,256]{4,3,2,1,0:T(8,128)(2,1)S(1)} %bitcast.8, bf16[256,256]{1,0:T(8,128)(2,1)S(1)} %copy-done.1), custom_call_target="tpu_custom_call" | custom-call | tf_op jit(solution)/shard_map/pallas_call | solution.py:236
  149.0 0.0 copy-start.2
  149.0 3.7 %shard_map.85 = bf16[96,128,256]{2,1,0:T(8,128)(2,1)S(1)} custom-call(s32[1,192]{1,0:T(1,128)S(1)} %bitcast.12, s32[1,192]{1,0:T(1,128)S(1)} %bitcast.14, s32[1,1]{1,0:T(1,128)S(6)} %copy.10.count_ref, bf16[96,128,256]{2,1,0:T(8,128)(2,1)S(1)} %bitcast.7, bf16[192,128,128]{2,1,0:T(8,128)(2,1)} %bitcast.16), custom_call_target="tpu_custom_call" | custom-call | flops 1610612736 | bytes 18874368 | tf_op jit(solution)/shard_map/pallas_call | solution.py:500
  152.7 0.0 copy-done.2
  152.7 36.8 %shard_map.86 = bf16[768,256]{1,0:T(8,128)(2,1)S(1)} custom-call(bf16[2,4,2,768,256]{4,3,2,1,0:T(8,128)(2,1)S(1)} %bitcast.9, bf16[256,256]{1,0:T(8,128)(2,1)S(1)} %copy-done.2), custom_call_target="tpu_custom_call" | custom-call | tf_op jit(solution)/shard_map/pallas_call | solution.py:424
  189.5 0.7 copy.11
Async XLA Ops:
  0.0 32.7 %copy-start.3 = (s32[1,1,192]{2,1,0:T(1,128)S(1)}, s32[1,1,192]{2,1,0:T(1,128)}, u32[]{:S(2)}) copy-start(s32[1,1,192]{2,1,0:T(1,128)} %param.11) | copy-start | bytes 2308
  0.0 32.7 %copy-start.4 = (s32[1,1,192]{2,1,0:T(1,128)S(1)}, s32[1,1,192]{2,1,0:T(1,128)}, u32[]{:S(2)}) copy-start(s32[1,1,192]{2,1,0:T(1,128)} %param.10) | copy-start | bytes 2308
  0.7 1.0 copy-start
  1.7 0.7 copy-start.5
  32.7 3.7 %copy-start.1 = (bf16[256,256]{1,0:T(8,128)(2,1)S(1)}, bf16[256,256]{1,0:T(8,128)(2,1)}, u32[]{:S(2)}) copy-start(bf16[256,256]{1,0:T(8,128)(2,1)} %weight.2) | copy-start | bytes 393220
  149.0 3.7 %copy-start.2 = (bf16[256,256]{1,0:T(8,128)(2,1)S(1)}, bf16[256,256]{1,0:T(8,128)(2,1)}, u32[]{:S(2)}) copy-start(bf16[256,256]{1,0:T(8,128)(2,1)} %weight.3) | copy-start | bytes 393220

commit v5 on v4

--- a/solution.py
+++ b/solution.py
@@ -8,7 +8,7 @@
 
 MESH = pl.DeviceIdType.MESH
 PARTS = 4
-LAGS = dict(r1=0, r2=1, r3=2, r4=3, r5=4, d=5, g2=5, g4=6, g3=6, g3o=6, g5=8, g4o=14, end=15)
+LAGS = dict(r1=0, r2=1, r3=2, r4=3, r5=4, d=5, g2=6, g4=6, g5=8, g3=7, g3o=7, g4o=9, end=12)
 
 
 class Mail:
@@ -33,10 +33,12 @@
             copy.wait_send()
 
 
-def greet(devices):
+def greet(devices, meanwhile=None):
     barrier = pltpu.get_barrier_semaphore()
     for device in devices:
         pl.semaphore_signal(barrier, inc=1, device_id=device, device_id_type=MESH)
+    if meanwhile is not None:
+        meanwhile()
     pl.semaphore_wait(barrier, len(devices))
 
 
@@ -252,7 +254,9 @@
     return out.reshape(16, slab, width)
 
 
-def gather_kernel(order, features, out, own, send_sem, recv_sem, own_sem):
+def gather_kernel(
+    order_hbm, features_hbm, out, order, features, own, send_sem, recv_sem, own_sem, load_sem
+):
     slab = features.shape[0]
     h = slab // 4
     me = lax.axis_index("col")
@@ -269,9 +273,19 @@
             preferred_element_type=jnp.float32,
         ).astype(own.dtype)
 
-    for q in (0, 2):
-        place(q)
-    greet((to_r, to_l, to_z, to_c))
+    def begin():
+        loads = (
+            pltpu.make_async_copy(features_hbm, features, load_sem.at[0]),
+            pltpu.make_async_copy(order_hbm, order, load_sem.at[1]),
+        )
+        for load in loads:
+            load.start()
+        for load in loads:
+            load.wait()
+        for q in (0, 2):
+            place(q)
+
+    greet((to_r, to_l, to_z, to_c), begin)
     mail = Mail(send_sem, recv_sem)
     whole, lower, upper = pl.ds(0, slab), pl.ds(0, 2 * h), pl.ds(2 * h, 2 * h)
 
@@ -341,17 +355,20 @@
 
 def col_gather(order, features):
     slab, width = features.shape
-    vmem = pl.BlockSpec(memory_space=pltpu.VMEM)
+    hbm = pl.BlockSpec(memory_space=pltpu.HBM)
     out = pl.pallas_call(
         gather_kernel,
         out_shape=jax.ShapeDtypeStruct((2, 4, 2, slab, width), features.dtype),
-        in_specs=[vmem, vmem],
-        out_specs=vmem,
+        in_specs=[hbm, hbm],
+        out_specs=pl.BlockSpec(memory_space=pltpu.VMEM),
         scratch_shapes=[
+            pltpu.VMEM(order.shape, order.dtype),
+            pltpu.VMEM((slab, width), features.dtype),
             pltpu.VMEM((slab, width), features.dtype),
             pltpu.SemaphoreType.DMA((45,)),
             pltpu.SemaphoreType.DMA((45,)),
             pltpu.SemaphoreType.DMA,
+            pltpu.SemaphoreType.DMA((2,)),
         ],
         compiler_params=pltpu.CompilerParams(
             collective_id=0, has_side_effects=True, vmem_limit_bytes=16 << 20

time: 191 us -> 186 us (0.974)
  Pallas kernels: 187 us -> 181 us
    pallas_call x1, Pallas kernels: 112 us -> 106 us  [row_exchange(): pl.pallas_call(row_kernel, out_shape=jax.ShapeDtypeStruct((2, 2, 4, slab,...]
where the time goes in v5:
time: 186 us; the launch traced here: 184 us
  Pallas kernels  181 us (97%)
  local copies, waits for them, and re-layouts  2.44 us (1%)
    pallas_call x1, Pallas kernels, row_exchange(): pl.pallas_call(row_kernel, out_shape=jax.ShapeDtypeStruct((2, 2, 4, slab,...  106 us
    pallas_call x1, Pallas kernels, col_sum(): pl.pallas_call(sum_kernel, out_shape=jax.ShapeDtypeStruct((slab, width),...  35.3 us
    pallas_call x1, Pallas kernels, col_gather(): pl.pallas_call(gather_kernel, out_shape=jax.ShapeDtypeStruct((2, 4, 2, sl...  29.9 us
    pallas_call x2, Pallas kernels, block_product(): pl.pallas_call(functools.partial(product_kernel, transposed, unroll), out...  9.23 us

profile of v5, /device:TPU:1, one launch (start us, length us, event | category | flops | bytes accessed | tf_op | source)
XLA Modules:
  0.0 184.1 jit_solution(8451533879666150218)
XLA Ops:
  0.0 0.0 copy-start.3
  0.0 0.0 copy-start.4
  0.7 0.0 copy-start
  0.7 1.0 copy-done
  1.7 0.0 copy-start.5
  1.7 0.7 copy-done.5
  2.4 29.9 %shard_map.82 = bf16[2,4,2,768,256]{4,3,2,1,0:T(8,128)(2,1)S(1)} custom-call(s32[1,768]{1,0:T(1,128)S(1)} %copy-done.5, bf16[768,256]{1,0:T(8,128)(2,1)S(1)} %copy-done), custom_call_target="tpu_custom_call" | custom-call | tf_op jit(solution)/shard_map/pallas_call | solution.py:359
  32.3 0.0 copy-done.3
  32.3 0.0 copy-done.4
  32.3 0.0 copy-start.1
  32.3 4.7 %shard_map.83 = bf16[96,128,256]{2,1,0:T(8,128)(2,1)S(1)} custom-call(s32[1,192]{1,0:T(1,128)S(1)} %bitcast.13, s32[1,192]{1,0:T(1,128)S(1)} %bitcast.11, s32[1,1]{1,0:T(1,128)S(6)} %copy.10.count_ref, bf16[96,128,256]{2,1,0:T(8,128)(2,1)S(1)} %bitcast.10, bf16[192,128,128]{2,1,0:T(8,128)(2,1)} %bitcast.15), custom_call_target="tpu_custom_call" | custom-call | flops 1610612736 | bytes 18874368 | tf_op jit(solution)/shard_map/pallas_call | solution.py:517
  37.0 0.0 copy-done.1
  37.0 106.4 %shard_map.84 = bf16[2,2,4,768,256]{4,3,2,1,0:T(8,128)(2,1)S(1)} custom-call(bf16[2,2,4,768,256]{4,3,2,1,0:T(8,128)(2,1)S(1)} %bitcast.8, bf16[256,256]{1,0:T(8,128)(2,1)S(1)} %copy-done.1), custom_call_target="tpu_custom_call" | custom-call | tf_op jit(solution)/shard_map/pallas_call | solution.py:238
  143.4 0.0 copy-start.2
  143.4 4.6 %shard_map.85 = bf16[96,128,256]{2,1,0:T(8,128)(2,1)S(1)} custom-call(s32[1,192]{1,0:T(1,128)S(1)} %bitcast.12, s32[1,192]{1,0:T(1,128)S(1)} %bitcast.14, s32[1,1]{1,0:T(1,128)S(6)} %copy.10.count_ref, bf16[96,128,256]{2,1,0:T(8,128)(2,1)S(1)} %bitcast.7, bf16[192,128,128]{2,1,0:T(8,128)(2,1)} %bitcast.16), custom_call_target="tpu_custom_call" | custom-call | flops 1610612736 | bytes 18874368 | tf_op jit(solution)/shard_map/pallas_call | solution.py:517
  148.0 0.0 copy-done.2
  148.0 35.3 %shard_map.86 = bf16[768,256]{1,0:T(8,128)(2,1)S(1)} custom-call(bf16[2,4,2,768,256]{4,3,2,1,0:T(8,128)(2,1)S(1)} %bitcast.9, bf16[256,256]{1,0:T(8,128)(2,1)S(1)} %copy-done.2), custom_call_target="tpu_custom_call" | custom-call | tf_op jit(solution)/shard_map/pallas_call | solution.py:441
  183.4 0.7 copy.11
Async XLA Ops:
  0.0 32.3 %copy-start.3 = (s32[1,1,192]{2,1,0:T(1,128)S(1)}, s32[1,1,192]{2,1,0:T(1,128)}, u32[]{:S(2)}) copy-start(s32[1,1,192]{2,1,0:T(1,128)} %param.11) | copy-start | bytes 2308
  0.0 32.3 %copy-start.4 = (s32[1,1,192]{2,1,0:T(1,128)S(1)}, s32[1,1,192]{2,1,0:T(1,128)}, u32[]{:S(2)}) copy-start(s32[1,1,192]{2,1,0:T(1,128)} %param.10) | copy-start | bytes 2308
  0.7 1.0 copy-start
  1.7 0.7 copy-start.5
  32.3 4.7 %copy-start.1 = (bf16[256,256]{1,0:T(8,128)(2,1)S(1)}, bf16[256,256]{1,0:T(8,128)(2,1)}, u32[]{:S(2)}) copy-start(bf16[256,256]{1,0:T(8,128)(2,1)} %weight.2) | copy-start | bytes 393220
  143.4 4.6 %copy-start.2 = (bf16[256,256]{1,0:T(8,128)(2,1)S(1)}, bf16[256,256]{1,0:T(8,128)(2,1)}, u32[]{:S(2)}) copy-start(bf16[256,256]{1,0:T(8,128)(2,1)} %weight.3) | copy-start | bytes 393220

commit v6 on v5

--- a/solution.py
+++ b/solution.py
@@ -254,6 +254,10 @@
     return out.reshape(16, slab, width)
 
 
+def tail_rows(slab):
+    return max(slab // 96, 1) * 16
+
+
 def gather_kernel(
     order_hbm, features_hbm, out, order, features, own, send_sem, recv_sem, own_sem, load_sem
 ):
@@ -287,7 +291,8 @@
 
     greet((to_r, to_l, to_z, to_c), begin)
     mail = Mail(send_sem, recv_sem)
-    whole, lower, upper = pl.ds(0, slab), pl.ds(0, 2 * h), pl.ds(2 * h, 2 * h)
+    whole, cut = pl.ds(0, slab), tail_rows(slab)
+    tail = pl.ds(slab - cut, cut)
 
     def send_own(name, q, to):
         rows = pl.ds(q * h, h)
@@ -298,6 +303,9 @@
 
     def quarter(q):
         return pl.ds(q * h, h)
+
+    def short(q):
+        return pl.ds(q * h, h - cut if q == 3 else h)
 
     for q in (0, 2):
         send_own("r" if q == 0 else "l", q, to_r if q == 0 else to_l)
@@ -321,20 +329,22 @@
     send_on(("fr", 1), zp, yl, quarter(1), to_r)
     mail.await_recv(("l", 3))
     send_on(("fl", 3), zp, yr, quarter(3), to_l)
+    send_on("tr", zp, yr, tail, to_z)
     for q in (0, 2):
         mail.await_recv(("z", q))
-        send_on(("pr", q), zq, y, quarter(q), to_r)
-        send_on(("pl", q), zq, y, quarter(q), to_l)
+        send_on(("pr", q), zq, y, short(q), to_r)
+        send_on(("pl", q), zq, y, short(q), to_l)
     mail.await_recv(("fr", 0))
     send_on(("zo", 0), zp, yo, quarter(0), to_z)
     mail.await_recv(("fl", 2))
     send_on(("zo", 2), zp, yo, quarter(2), to_z)
     for q in (1, 3):
         mail.await_recv(("z", q))
-        send_on(("pr", q), zq, y, quarter(q), to_r)
-        send_on(("pl", q), zq, y, quarter(q), to_l)
+        send_on(("pr", q), zq, y, short(q), to_r)
+        send_on(("pl", q), zq, y, short(q), to_l)
     send_on("c1", zq, y, whole, to_c)
     mail.await_recv(("r", 2), ("r", 3), ("l", 0), ("l", 1))
+    send_on("tl", zp, yl, tail, to_z)
     send_on("c2", zp, yl, whole, to_c)
     send_on("c3", zp, yr, whole, to_c)
     mail.await_recv(("fr", 1))
@@ -347,7 +357,12 @@
         for name, zs, ys in (("pr", zq, yl), ("pl", zq, yr), ("zo", zq, yo)):
             mail.await_recv((name, q))
             last.append(("c" + name, q))
-            send_on(last[-1], zs, ys, quarter(q), to_c)
+            send_on(last[-1], zs, ys, quarter(q) if name == "zo" else short(q), to_c)
+        if q == 1:
+            for name, ys in (("tr", yr), ("tl", yl)):
+                mail.await_recv(name)
+                last.append("c" + name)
+                send_on(last[-1], zq, ys, tail, to_c)
     own_copy.wait()
     mail.await_recv("c0", "c1", "c2", "c3", "c4", *last)
     mail.finish()
@@ -365,8 +380,8 @@
             pltpu.VMEM(order.shape, order.dtype),
             pltpu.VMEM((slab, width), features.dtype),
             pltpu.VMEM((slab, width), features.dtype),
-            pltpu.SemaphoreType.DMA((45,)),
-            pltpu.SemaphoreType.DMA((45,)),
+            pltpu.SemaphoreType.DMA((49,)),
+            pltpu.SemaphoreType.DMA((49,)),
             pltpu.SemaphoreType.DMA,
             pltpu.SemaphoreType.DMA((2,)),
         ],
@@ -379,7 +394,7 @@
 
 def sum_kernel(
     part, weight, out, sib, both, z1, s2_l, s2_r, s3_l, s3_r, opp, s4b_l, s4b_r, s4a_l, s4a_r,
-    c_r, c_l, via, z2, send_sem, recv_sem,
+    c_r, c_l, z2, t_r, t_l, send_sem, recv_sem,
 ):
     slab = part.shape[3]
     h = slab // 2
@@ -389,10 +404,16 @@
     to_r, to_l = {"col": zp * 8 + yr * 2 + c}, {"col": zp * 8 + yl * 2 + c}
     to_z, to_c = {"col": zq * 8 + y * 2 + c}, {"col": zp * 8 + y * 2 + d}
     a, b = pl.ds(0, h), pl.ds(h, h)
+    cut = tail_rows(slab)
+    head, tail = pl.ds(0, slab - cut), pl.ds(slab - cut, cut)
     dests = ((zq, yo), (zq, yr), (zq, yl), (zp, yr), (zp, yl), (zp, yo), (zq, y), (zp, y))
     greet((to_r, to_l, to_z, to_c))
     mail = Mail(send_sem, recv_sem)
-    for i, (zs, ys) in enumerate(dests):
+    quarters = [pl.ds(q * (h // 2), h // 2) for q in range(4)]
+    turns = (0, 2, 1, 3)
+    for q in turns:
+        mail.send(("c0", q), part.at[zq, yo, d, quarters[q]], sib.at[0, quarters[q]], to_c)
+    for i, (zs, ys) in enumerate(dests[1:], 1):
         mail.send(("c", i), part.at[zs, ys, d], sib.at[i], to_c)
 
     def join(i):
@@ -400,42 +421,55 @@
         mail.await_recv(("c", i))
         add_rows(both.at[i], (part.at[zs, ys, c], sib.at[i]))
 
-    join(0)
-    mail.send("z1", both.at[0], z1, to_z)
+    for q in turns:
+        rows = quarters[q]
+        mail.await_recv(("c0", q))
+        add_rows(both.at[0, rows], (part.at[zq, yo, c, rows], sib.at[0, rows]))
+        mail.send(("z1", q), both.at[0, rows], z1.at[rows], to_z)
     join(1)
-    mail.send("s2r", both.at[1], s2_l, to_r)
+    mail.send("s2r", both.at[1, head], s2_l, to_r)
     join(2)
-    mail.send("s2l", both.at[2], s2_r, to_l)
-    join(3)
+    mail.send("s2l", both.at[2, head], s2_r, to_l)
+    mail.send("tr", both.at[1, tail], t_r, to_z)
+    mail.send("tl", both.at[2, tail], t_l, to_z)
+    for i in (5, 3, 4, 6, 7):
+        join(i)
+    for q in turns:
+        rows, half = quarters[q], quarters[q % 2]
+        mail.await_recv(("z1", q))
+        add_rows(opp.at[rows], (both.at[5, rows], z1.at[rows]))
+        if q < 2:
+            mail.send(("s3r", q), opp.at[rows], s3_l.at[half], to_r)
+        else:
+            mail.send(("s3l", q), opp.at[rows], s3_r.at[half], to_l)
+    mail.await_recv("tr", "tl")
+    add_rows(both.at[3, tail], (both.at[3, tail], t_r))
+    add_rows(both.at[4, tail], (both.at[4, tail], t_l))
     mail.send("s4br", both.at[3, b], s4b_l, to_r)
-    join(4)
     mail.send("s4bl", both.at[4, a], s4b_r, to_l)
-    join(5)
-    mail.await_recv("z1")
-    add_rows(opp, (both.at[5], z1))
-    mail.send("s3r", opp.at[a], s3_l, to_r)
-    mail.send("s3l", opp.at[b], s3_r, to_l)
-    join(6)
-    join(7)
     mail.await_recv("s2r", "s2l")
-    add_rows(via, (both.at[6], s2_l, s2_r))
-    mail.send("z2", via, z2, to_z)
-    mail.await_recv("s3r")
-    add_rows(c_r, (both.at[3, a], s3_l))
-    mail.send("s4ar", c_r, s4a_l, to_r)
-    mail.await_recv("s3l")
-    add_rows(c_l, (both.at[4, b], s3_r))
-    mail.send("s4al", c_l, s4a_r, to_l)
-    mail.await_recv("z2", "s4bl", "s4ar")
+    add_rows(both.at[6, head], (both.at[6, head], s2_l, s2_r))
+    mail.send("z2", both.at[6], z2, to_z)
+    for q in turns:
+        rows, half = quarters[q], quarters[q % 2]
+        if q < 2:
+            mail.await_recv(("s3r", q))
+            add_rows(c_r.at[half], (both.at[3, rows], s3_l.at[half]))
+            mail.send(("s4ar", q), c_r.at[half], s4a_l.at[half], to_r)
+        else:
+            mail.await_recv(("s3l", q))
+            add_rows(c_l.at[half], (both.at[4, rows], s3_r.at[half]))
+            mail.send(("s4al", q), c_l.at[half], s4a_r.at[half], to_l)
+    mail.await_recv("z2", "s4bl", ("s4ar", 0), ("s4ar", 1))
     dense_relu(out.at[a], (both.at[7, a], s4a_l, s4b_r, z2.at[a]), weight)
-    mail.await_recv("s4br", "s4al")
+    mail.await_recv("s4br", ("s4al", 2), ("s4al", 3))
     dense_relu(out.at[b], (both.at[7, b], s4b_l, s4a_r, z2.at[b]), weight)
     mail.finish()
 
 
 def col_sum(part, weight):
     _, slab, width = part.shape
-    dt, h = part.dtype, slab // 2
+    dt, h, cut = part.dtype, slab // 2, tail_rows(slab)
     vmem = pl.BlockSpec(memory_space=pltpu.VMEM)
     full, half = pltpu.VMEM((slab, width), dt), pltpu.VMEM((h, width), dt)
     return pl.pallas_call(
@@ -445,8 +479,9 @@
         out_specs=vmem,
         scratch_shapes=(
             [pltpu.VMEM((8, slab, width), dt)] * 2
-            + [full] * 3 + [half] * 2 + [full] + [half] * 6 + [full] * 2
-            + [pltpu.SemaphoreType.DMA((18,))] * 2
+            + [full] + [pltpu.VMEM((slab - cut, width), dt)] * 2 + [half] * 2 + [full] + [half] * 6
+            + [full] + [pltpu.VMEM((cut, width), dt)] * 2
+            + [pltpu.SemaphoreType.DMA((30,))] * 2
         ),
         compiler_params=pltpu.CompilerParams(
             collective_id=2, has_side_effects=True, vmem_limit_bytes=28 << 20
@@ -454,7 +489,7 @@
     )(part.reshape(2, 4, 2, slab, width), weight)
 
 
-CHUNK = 16
+CHUNK = 32
 
 
 def product_kernel(
@@ -509,7 +544,7 @@
         out[g] = total[g].astype(out.dtype)
 
 
-def block_product(panel, tiles, source_ids, target_ids, count, transposed, unroll=16):
+def block_product(panel, tiles, source_ids, target_ids, count, transposed, unroll=32):
     slots, block, _ = tiles.shape
     blocks, _, width = panel.shape
     smem = pl.BlockSpec(memory_space=pltpu.SMEM)

time: 186 us -> 183 us (0.984)
  Pallas kernels: 181 us -> 179 us
where the time goes in v6:
time: 183 us
  Pallas kernels  179 us (98%)
  local copies, waits for them, and re-layouts  2.44 us (1%)
    pallas_call x1, Pallas kernels, row_exchange(): pl.pallas_call(row_kernel, out_shape=jax.ShapeDtypeStruct((2, 2, 4, slab,...  107 us
    pallas_call x1, Pallas kernels, col_sum(): pl.pallas_call(sum_kernel, out_shape=jax.ShapeDtypeStruct((slab, width),...  33.5 us
    pallas_call x1, Pallas kernels, col_gather(): pl.pallas_call(gather_kernel, out_shape=jax.ShapeDtypeStruct((2, 4, 2, sl...  28.6 us
    pallas_call x2, Pallas kernels, block_product(): pl.pallas_call(functools.partial(product_kernel, transposed, unroll), out...  10.2 us

profile of v6, /device:TPU:1, one launch (start us, length us, event | category | flops | bytes accessed | tf_op | source)
XLA Modules:
  0.0 182.6 jit_solution(15034788860443797286)
XLA Ops:
  0.0 0.0 copy-start.3
  0.0 0.0 copy-start.4
  0.7 0.0 copy-start
  0.7 1.0 copy-done
  1.7 0.0 copy-start.5
  1.7 0.7 copy-done.5
  2.4 28.6 %shard_map.82 = bf16[2,4,2,768,256]{4,3,2,1,0:T(8,128)(2,1)S(1)} custom-call(s32[1,768]{1,0:T(1,128)S(1)} %copy-done.5, bf16[768,256]{1,0:T(8,128)(2,1)S(1)} %copy-done), custom_call_target="tpu_custom_call" | custom-call | tf_op jit(solution)/shard_map/pallas_call | solution.py:374
  31.0 0.0 copy-done.3
  31.0 0.0 copy-done.4
  31.0 0.0 copy-start.1
  31.0 5.1 %shard_map.83 = bf16[96,128,256]{2,1,0:T(8,128)(2,1)S(1)} custom-call(s32[1,192]{1,0:T(1,128)S(1)} %bitcast.13, s32[1,192]{1,0:T(1,128)S(1)} %bitcast.11, s32[1,1]{1,0:T(1,128)S(6)} %copy.10.count_ref, bf16[96,128,256]{2,1,0:T(8,128)(2,1)S(1)} %bitcast.10, bf16[192,128,128]{2,1,0:T(8,128)(2,1)} %bitcast.15), custom_call_target="tpu_custom_call" | custom-call | flops 1610612736 | bytes 18874368 | tf_op jit(solution)/shard_map/pallas_call | solution.py:552
  36.1 0.0 copy-done.1
  36.1 107.0 %shard_map.84 = bf16[2,2,4,768,256]{4,3,2,1,0:T(8,128)(2,1)S(1)} custom-call(bf16[2,2,4,768,256]{4,3,2,1,0:T(8,128)(2,1)S(1)} %bitcast.8, bf16[256,256]{1,0:T(8,128)(2,1)S(1)} %copy-done.1), custom_call_target="tpu_custom_call" | custom-call | tf_op jit(solution)/shard_map/pallas_call | solution.py:238
  143.1 0.0 copy-start.2
  143.1 5.2 %shard_map.85 = bf16[96,128,256]{2,1,0:T(8,128)(2,1)S(1)} custom-call(s32[1,192]{1,0:T(1,128)S(1)} %bitcast.12, s32[1,192]{1,0:T(1,128)S(1)} %bitcast.14, s32[1,1]{1,0:T(1,128)S(6)} %copy.10.count_ref, bf16[96,128,256]{2,1,0:T(8,128)(2,1)S(1)} %bitcast.7, bf16[192,128,128]{2,1,0:T(8,128)(2,1)} %bitcast.16), custom_call_target="tpu_custom_call" | custom-call | flops 1610612736 | bytes 18874368 | tf_op jit(solution)/shard_map/pallas_call | solution.py:552
  148.3 0.0 copy-done.2
  148.3 33.5 %shard_map.86 = bf16[768,256]{1,0:T(8,128)(2,1)S(1)} custom-call(bf16[2,4,2,768,256]{4,3,2,1,0:T(8,128)(2,1)S(1)} %bitcast.9, bf16[256,256]{1,0:T(8,128)(2,1)S(1)} %copy-done.2), custom_call_target="tpu_custom_call" | custom-call | tf_op jit(solution)/shard_map/pallas_call | solution.py:475
  181.8 0.7 copy.11
Async XLA Ops:
  0.0 31.0 %copy-start.3 = (s32[1,1,192]{2,1,0:T(1,128)S(1)}, s32[1,1,192]{2,1,0:T(1,128)}, u32[]{:S(2)}) copy-start(s32[1,1,192]{2,1,0:T(1,128)} %param.11) | copy-start | bytes 2308
  0.0 31.0 %copy-start.4 = (s32[1,1,192]{2,1,0:T(1,128)S(1)}, s32[1,1,192]{2,1,0:T(1,128)}, u32[]{:S(2)}) copy-start(s32[1,1,192]{2,1,0:T(1,128)} %param.10) | copy-start | bytes 2308
  0.7 1.0 copy-start
  1.7 0.7 copy-start.5
  31.0 5.1 %copy-start.1 = (bf16[256,256]{1,0:T(8,128)(2,1)S(1)}, bf16[256,256]{1,0:T(8,128)(2,1)}, u32[]{:S(2)}) copy-start(bf16[256,256]{1,0:T(8,128)(2,1)} %weight.2) | copy-start | bytes 393220
  143.1 5.2 %copy-start.2 = (bf16[256,256]{1,0:T(8,128)(2,1)S(1)}, bf16[256,256]{1,0:T(8,128)(2,1)}, u32[]{:S(2)}) copy-start(bf16[256,256]{1,0:T(8,128)(2,1)} %weight.3) | copy-start | bytes 393220

commit v7 on v6

--- a/solution.py
+++ b/solution.py
@@ -8,7 +8,15 @@
 
 MESH = pl.DeviceIdType.MESH
 PARTS = 4
-LAGS = dict(r1=0, r2=1, r3=2, r4=3, r5=4, d=5, g2=6, g4=6, g5=8, g3=7, g3o=7, g4o=9, end=12)
+ORDER = (
+    ("r1z", 0), ("r1o", 0), ("r1z", 2), ("r1z", 3), ("r1x", 0), ("r2", 0), ("r1o", 3), ("r1o", 2),
+    ("r2", 2), ("r3", 0), ("r1z", 1), ("r1x", 2), ("r3", 2), ("r4", 0), ("r2", 3), ("r1o", 1),
+    ("r1x", 3), ("r5", 0), ("r2", 1), ("r4", 2), ("r3", 3), ("d", 0), ("r5", 2), ("r1x", 1),
+    ("r3", 1), ("g2", 0), ("r4", 3), ("d", 2), ("g3o", 0), ("r5", 3), ("g2", 2), ("g4", 2),
+    ("r4", 1), ("g4", 0), ("g4o", 0), ("g3", 0), ("d", 3), ("g3o", 2), ("r5", 1), ("g2", 3),
+    ("g3", 2), ("g4", 3), ("g5", 2), ("d", 1), ("g3o", 3), ("g5", 3), ("g3", 3), ("g2", 1),
+    ("g4", 1), ("g5", 0), ("g3", 1), ("g4o", 2), ("g3o", 1), ("g5", 1), ("g4o", 3), ("g4o", 1),
+)
 
 
 class Mail:
@@ -88,12 +96,18 @@
     def rows(p):
         return pl.ds(p * n, n), pl.ds(p * n, h), pl.ds(p * n + h, h)
 
-    def r1(p):
+    def r1z(p):
         n_, a, b = rows(p)
         mail.send(("r1r", p), at(part, zr, xo, n_), r1_l.at[p], to_zr)
         mail.send(("r1l", p), at(part, zl, xo, n_), r1_r.at[p], to_zl)
+
+    def r1o(p):
+        n_, a, b = rows(p)
         mail.send(("r2or", p), at(part, zo, xo, a), r2o_l.at[p], to_xr)
         mail.send(("r2ol", p), at(part, zo, xo, b), r2o_r.at[p], to_xl)
+
+    def r1x(p):
+        n_, a, b = rows(p)
         mail.send(("r3mr", p), part.at[:, other, xr, n_], r3m_l.at[p], to_xr)
         mail.send(("r3ml", p), part.at[:, other, xl, n_], r3m_r.at[p], to_xl)
         mail.send(("r3br", p), part.at[:, same, xr, b], r3b_l.at[p], to_xr)
@@ -213,14 +227,13 @@
         )))
 
     stages = dict(
-        r1=r1, r2=r2, r3=r3, r4=r4, r5=r5, d=dense, g2=g2, g4=g4, g5=g5, g3=g3, g3o=g3o, g4o=g4o,
-        end=end,
+        r1z=r1z, r1o=r1o, r1x=r1x, r2=r2, r3=r3, r4=r4, r5=r5, d=dense, g2=g2, g4=g4, g5=g5, g3=g3,
+        g3o=g3o, g4o=g4o,
     )
-    order = sorted(stages, key=lambda name: -LAGS[name])
-    for tick in range(PARTS + max(LAGS.values())):
-        for name in order:
-            if 0 <= tick - LAGS[name] < PARTS:
-                stages[name](tick - LAGS[name])
+    for name, p in ORDER:
+        stages[name](p)
+    for p in range(PARTS):
+        end(p)
     mail.finish()
 
 

time: 183 us -> 175 us (0.956); the launches traced: 183 us -> 173 us
  Pallas kernels: 179 us -> 170 us
    pallas_call x1, Pallas kernels: 107 us -> 103 us  [row_exchange(): pl.pallas_call(row_kernel, out_shape=jax.ShapeDtypeStruct((2, 2, 4, slab,...]
    pallas_call x2, Pallas kernels: 10.2 us -> 7.18 us  [block_product(): pl.pallas_call(functools.partial(product_kernel, transposed, unroll), out...]
    pallas_call x1, Pallas kernels: 33.5 us -> 30.9 us  [col_sum(): pl.pallas_call(sum_kernel, out_shape=jax.ShapeDtypeStruct((slab, width),...]
where the time goes in v7:
time: 175 us; the launch traced here: 173 us
  Pallas kernels  170 us (97%)
  local copies, waits for them, and re-layouts  2.44 us (1%)
    pallas_call x1, Pallas kernels, row_exchange(): pl.pallas_call(row_kernel, out_shape=jax.ShapeDtypeStruct((2, 2, 4, slab,...  103 us
    pallas_call x1, Pallas kernels, col_sum(): pl.pallas_call(sum_kernel, out_shape=jax.ShapeDtypeStruct((slab, width),...  30.9 us
    pallas_call x1, Pallas kernels, col_gather(): pl.pallas_call(gather_kernel, out_shape=jax.ShapeDtypeStruct((2, 4, 2, sl...  28.6 us
    pallas_call x2, Pallas kernels, block_product(): pl.pallas_call(functools.partial(product_kernel, transposed, unroll), out...  7.18 us

profile of v7, /device:TPU:1, one launch (start us, length us, event | category | flops | bytes accessed | tf_op | source)
XLA Modules:
  0.0 172.7 jit_solution(3961728412950462348)
XLA Ops:
  0.0 0.0 copy-start.3
  0.0 0.0 copy-start.4
  0.7 0.0 copy-start
  0.7 1.0 copy-done
  1.7 0.0 copy-start.5
  1.7 0.7 copy-done.5
  2.4 28.6 %shard_map.82 = bf16[2,4,2,768,256]{4,3,2,1,0:T(8,128)(2,1)S(1)} custom-call(s32[1,768]{1,0:T(1,128)S(1)} %copy-done.5, bf16[768,256]{1,0:T(8,128)(2,1)S(1)} %copy-done), custom_call_target="tpu_custom_call" | custom-call | tf_op jit(solution)/shard_map/pallas_call | solution.py:387
  31.0 0.0 copy-done.3
  31.0 0.0 copy-done.4
  31.0 0.0 copy-start.1
  31.0 3.6 %shard_map.83 = bf16[96,128,256]{2,1,0:T(8,128)(2,1)S(1)} custom-call(s32[1,192]{1,0:T(1,128)S(1)} %bitcast.13, s32[1,192]{1,0:T(1,128)S(1)} %bitcast.11, s32[1,1]{1,0:T(1,128)S(6)} %copy.10.count_ref, bf16[96,128,256]{2,1,0:T(8,128)(2,1)S(1)} %bitcast.10, bf16[192,128,128]{2,1,0:T(8,128)(2,1)} %bitcast.15), custom_call_target="tpu_custom_call" | custom-call | flops 1610612736 | bytes 18874368 | tf_op jit(solution)/shard_map/pallas_call | solution.py:565
  34.6 0.0 copy-done.1
  34.6 102.8 %shard_map.84 = bf16[2,2,4,768,256]{4,3,2,1,0:T(8,128)(2,1)S(1)} custom-call(bf16[2,2,4,768,256]{4,3,2,1,0:T(8,128)(2,1)S(1)} %bitcast.8, bf16[256,256]{1,0:T(8,128)(2,1)S(1)} %copy-done.1), custom_call_target="tpu_custom_call" | custom-call | tf_op jit(solution)/shard_map/pallas_call | solution.py:251
  137.4 0.0 copy-start.2
  137.4 3.6 %shard_map.85 = bf16[96,128,256]{2,1,0:T(8,128)(2,1)S(1)} custom-call(s32[1,192]{1,0:T(1,128)S(1)} %bitcast.12, s32[1,192]{1,0:T(1,128)S(1)} %bitcast.14, s32[1,1]{1,0:T(1,128)S(6)} %copy.10.count_ref, bf16[96,128,256]{2,1,0:T(8,128)(2,1)S(1)} %bitcast.7, bf16[192,128,128]{2,1,0:T(8,128)(2,1)} %bitcast.16), custom_call_target="tpu_custom_call" | custom-call | flops 1610612736 | bytes 18874368 | tf_op jit(solution)/shard_map/pallas_call | solution.py:565
  141.1 0.0 copy-done.2
  141.1 30.9 %shard_map.86 = bf16[768,256]{1,0:T(8,128)(2,1)S(1)} custom-call(bf16[2,4,2,768,256]{4,3,2,1,0:T(8,128)(2,1)S(1)} %bitcast.9, bf16[256,256]{1,0:T(8,128)(2,1)S(1)} %copy-done.2), custom_call_target="tpu_custom_call" | custom-call | tf_op jit(solution)/shard_map/pallas_call | solution.py:488
  172.0 0.7 copy.11
Async XLA Ops:
  0.0 31.0 %copy-start.3 = (s32[1,1,192]{2,1,0:T(1,128)S(1)}, s32[1,1,192]{2,1,0:T(1,128)}, u32[]{:S(2)}) copy-start(s32[1,1,192]{2,1,0:T(1,128)} %param.11) | copy-start | bytes 2308
  0.0 31.0 %copy-start.4 = (s32[1,1,192]{2,1,0:T(1,128)S(1)}, s32[1,1,192]{2,1,0:T(1,128)}, u32[]{:S(2)}) copy-start(s32[1,1,192]{2,1,0:T(1,128)} %param.10) | copy-start | bytes 2308
  0.7 1.0 copy-start
  1.7 0.7 copy-start.5
  31.0 3.6 %copy-start.1 = (bf16[256,256]{1,0:T(8,128)(2,1)S(1)}, bf16[256,256]{1,0:T(8,128)(2,1)}, u32[]{:S(2)}) copy-start(bf16[256,256]{1,0:T(8,128)(2,1)} %weight.2) | copy-start | bytes 393220
  137.4 3.6 %copy-start.2 = (bf16[256,256]{1,0:T(8,128)(2,1)S(1)}, bf16[256,256]{1,0:T(8,128)(2,1)}, u32[]{:S(2)}) copy-start(bf16[256,256]{1,0:T(8,128)(2,1)} %weight.3) | copy-start | bytes 393220

commit v8 on v7

--- a/solution.py
+++ b/solution.py
@@ -63,6 +63,16 @@
         out[at] = total.astype(out.dtype)
 
 
+def round_slab(out, total, slab):
+    block = total.shape[1]
+    count = out.shape[0] // block
+
+    @pl.loop(0, count)
+    def _(j):
+        at = pl.ds(pl.multiple_of(j * block, block), block)
+        out[at] = total[slab * count + j].astype(out.dtype)
+
+
 def dense_relu(out, terms, weight):
     total = terms[0][...].astype(jnp.float32)
     for term in terms[1:]:
@@ -72,7 +82,7 @@
 
 
 def row_kernel(
-    part, weight, out, r1_l, r1_r, cz, r2_l, r2_r, r2o_l, r2o_r, cx_r, cx_l, r3m_l, r3m_r,
+    total, weight, out, part, r1_l, r1_r, cz, r2_l, r2_r, r2o_l, r2o_r, cx_r, cx_l, r3m_l, r3m_r,
     r3b_l, r3a_r, r3a_l, r3b_r, sx, r4_l, r4_r, r5b_l, r5a_r, r5a_l, r5b_r, cs_r, cs_l, hid,
     send_sem, recv_sem, hid_sem,
 ):
@@ -90,7 +100,13 @@
     def at(ref, zs, xs, rows):
         return ref.at[zs // 2, zs % 2, xs, rows]
 
-    greet((to_xr, to_xl, to_zr, to_zl))
+
+    def round_x(*xs):
+        for zs in (zr, zl, zo, z):
+            for x_ in xs:
+                round_slab(part.at[zs // 2, zs % 2, x_], total, zs * 4 + x_)
+
+    greet((to_xr, to_xl, to_zr, to_zl), lambda: round_x(xo))
     mail = Mail(send_sem, recv_sem)
 
     def rows(p):
@@ -230,18 +246,23 @@
         r1z=r1z, r1o=r1o, r1x=r1x, r2=r2, r3=r3, r4=r4, r5=r5, d=dense, g2=g2, g4=g4, g5=g5, g3=g3,
         g3o=g3o, g4o=g4o,
     )
-    for name, p in ORDER:
+    first_x = next(i for i, (name, _) in enumerate(ORDER) if name == "r1x")
+    for i, (name, p) in enumerate(ORDER):
+        if i == first_x:
+            round_x(xr, xl)
         stages[name](p)
+        if i == first_x:
+            round_x(x)
     for p in range(PARTS):
         end(p)
     mail.finish()
 
 
-def row_exchange(part, weight):
-    _, slab, width = part.shape
+def row_exchange(total, weight, slab):
+    width = total.shape[2]
     n = slab // PARTS
     h = n // 2
-    dt = part.dtype
+    dt = weight.dtype
     vmem = pl.BlockSpec(memory_space=pltpu.VMEM)
     count = 40 * PARTS
 
@@ -254,16 +275,17 @@
         in_specs=[vmem, vmem],
         out_specs=vmem,
         scratch_shapes=(
-            buf(n) * 3 + buf(h) * 4 + buf(2, h) * 2 + buf(2, n) * 2 + buf(2, h) * 4
+            [pltpu.VMEM((2, 2, 4, slab, width), dt)]
+            + buf(n) * 3 + buf(h) * 4 + buf(2, h) * 2 + buf(2, n) * 2 + buf(2, h) * 4
             + buf(2, 2, n) + buf(h) * 8
             + [pltpu.VMEM((slab, width), dt)]
             + [pltpu.SemaphoreType.DMA((count,))] * 2
             + [pltpu.SemaphoreType.DMA((PARTS,))]
         ),
         compiler_params=pltpu.CompilerParams(
-            collective_id=1, has_side_effects=True, vmem_limit_bytes=28 << 20
+            collective_id=1, has_side_effects=True, vmem_limit_bytes=20 << 20
         ),
-    )(part.reshape(2, 2, 4, slab, width), weight)
+    )(total, weight)
     return out.reshape(16, slab, width)
 
 
@@ -271,9 +293,7 @@
     return max(slab // 96, 1) * 16
 
 
-def gather_kernel(
-    order_hbm, features_hbm, out, order, features, own, send_sem, recv_sem, own_sem, load_sem
-):
+def gather_kernel(order, features, out, own, send_sem, recv_sem, own_sem):
     slab = features.shape[0]
     h = slab // 4
     me = lax.axis_index("col")
@@ -291,14 +311,6 @@
         ).astype(own.dtype)
 
     def begin():
-        loads = (
-            pltpu.make_async_copy(features_hbm, features, load_sem.at[0]),
-            pltpu.make_async_copy(order_hbm, order, load_sem.at[1]),
-        )
-        for load in loads:
-            load.start()
-        for load in loads:
-            load.wait()
         for q in (0, 2):
             place(q)
 
@@ -383,34 +395,33 @@
 
 def col_gather(order, features):
     slab, width = features.shape
-    hbm = pl.BlockSpec(memory_space=pltpu.HBM)
+    vmem = pl.BlockSpec(memory_space=pltpu.VMEM)
     out = pl.pallas_call(
         gather_kernel,
         out_shape=jax.ShapeDtypeStruct((2, 4, 2, slab, width), features.dtype),
-        in_specs=[hbm, hbm],
-        out_specs=pl.BlockSpec(memory_space=pltpu.VMEM),
+        in_specs=[vmem, vmem],
+        out_specs=vmem,
         scratch_shapes=[
-            pltpu.VMEM(order.shape, order.dtype),
-            pltpu.VMEM((slab, width), features.dtype),
             pltpu.VMEM((slab, width), features.dtype),
             pltpu.SemaphoreType.DMA((49,)),
             pltpu.SemaphoreType.DMA((49,)),
             pltpu.SemaphoreType.DMA,
-            pltpu.SemaphoreType.DMA((2,)),
         ],
         compiler_params=pltpu.CompilerParams(
-            collective_id=0, has_side_effects=True, vmem_limit_bytes=16 << 20
+            collective_id=0, has_side_effects=True, vmem_limit_bytes=12 << 20
         ),
     )(order, features)
     return out.reshape(16, slab, width)
 
 
 def sum_kernel(
-    part, weight, out, sib, both, z1, s2_l, s2_r, s3_l, s3_r, opp, s4b_l, s4b_r, s4a_l, s4a_r,
+    total, weight, out, mine, sib, both, z1, s2_l, s2_r, s3_l, s3_r, opp, s4b_l, s4b_r, s4a_l, s4a_r,
     c_r, c_l, z2, t_r, t_l, send_sem, recv_sem,
 ):
-    slab = part.shape[3]
+    slab = out.shape[0]
     h = slab // 2
+    block = total.shape[1]
+    count = slab // block
     me = lax.axis_index("col")
     zp, y, c = me // 8, (me // 2) % 4, me % 2
     yr, yl, yo, zq, d = (y + 1) % 4, (y + 3) % 4, (y + 2) % 4, 1 - zp, 1 - c
@@ -424,21 +435,38 @@
     mail = Mail(send_sem, recv_sem)
     quarters = [pl.ds(q * (h // 2), h // 2) for q in range(4)]
     turns = (0, 2, 1, 3)
+
+    def slab_of(i, core):
+        zs, ys = dests[i]
+        return (zs * 4 + ys) * 2 + core
+
+    def give(i):
+        round_slab(mine.at[i], total, slab_of(i, d))
+        if i > 0:
+            mail.send(("c", i), mine.at[i], sib.at[i], to_c)
+
+    def join(i):
+        if i > 0:
+            mail.await_recv(("c", i))
+
+        @pl.loop(0, count)
+        def _(j):
+            at = pl.ds(pl.multiple_of(j * block, block), block)
+            both[i, at] = (
+                total[slab_of(i, c) * count + j] + sib[i, at].astype(jnp.float32)
+            ).astype(both.dtype)
+
+    give(0)
     for q in turns:
-        mail.send(("c0", q), part.at[zq, yo, d, quarters[q]], sib.at[0, quarters[q]], to_c)
-    for i, (zs, ys) in enumerate(dests[1:], 1):
-        mail.send(("c", i), part.at[zs, ys, d], sib.at[i], to_c)
-
-    def join(i):
-        zs, ys = dests[i]
-        mail.await_recv(("c", i))
-        add_rows(both.at[i], (part.at[zs, ys, c], sib.at[i]))
-
+        mail.send(("c0", q), mine.at[0, quarters[q]], sib.at[0, quarters[q]], to_c)
+    for i in (1, 2):
+        give(i)
+    mail.await_recv(*(("c0", q) for q in turns))
+    join(0)
     for q in turns:
-        rows = quarters[q]
-        mail.await_recv(("c0", q))
-        add_rows(both.at[0, rows], (part.at[zq, yo, c, rows], sib.at[0, rows]))
-        mail.send(("z1", q), both.at[0, rows], z1.at[rows], to_z)
+        mail.send(("z1", q), both.at[0, quarters[q]], z1.at[quarters[q]], to_z)
+    for i in (5, 3, 4, 6, 7):
+        give(i)
     join(1)
     mail.send("s2r", both.at[1, head], s2_l, to_r)
     join(2)
@@ -473,16 +501,20 @@
             mail.await_recv(("s3l", q))
             add_rows(c_l.at[half], (both.at[4, rows], s3_r.at[half]))
             mail.send(("s4al", q), c_l.at[half], s4a_r.at[half], to_l)
-    mail.await_recv("z2", "s4bl", ("s4ar", 0), ("s4ar", 1))
-    dense_relu(out.at[a], (both.at[7, a], s4a_l, s4b_r, z2.at[a]), weight)
-    mail.await_recv("s4br", ("s4al", 2), ("s4al", 3))
-    dense_relu(out.at[b], (both.at[7, b], s4b_l, s4a_r, z2.at[b]), weight)
+    mail.await_recv("s4bl", "s4br", "z2")
+    for q in turns:
+        rows, half = quarters[q], quarters[q % 2]
+        mail.await_recv(("s4ar" if q < 2 else "s4al", q))
+        near = (s4a_l, s4b_r) if q < 2 else (s4a_r, s4b_l)
+        dense_relu(
+            out.at[rows], (both.at[7, rows], near[0].at[half], near[1].at[half], z2.at[rows]), weight
+        )
     mail.finish()
 
 
-def col_sum(part, weight):
-    _, slab, width = part.shape
-    dt, h, cut = part.dtype, slab // 2, tail_rows(slab)
+def col_sum(total, weight, slab):
+    width = total.shape[2]
+    dt, h, cut = weight.dtype, slab // 2, tail_rows(slab)
     vmem = pl.BlockSpec(memory_space=pltpu.VMEM)
     full, half = pltpu.VMEM((slab, width), dt), pltpu.VMEM((h, width), dt)
     return pl.pallas_call(
@@ -491,35 +523,26 @@
         in_specs=[vmem, vmem],
         out_specs=vmem,
         scratch_shapes=(
-            [pltpu.VMEM((8, slab, width), dt)] * 2
+            [pltpu.VMEM((8, slab, width), dt)] * 3
             + [full] + [pltpu.VMEM((slab - cut, width), dt)] * 2 + [half] * 2 + [full] + [half] * 6
             + [full] + [pltpu.VMEM((cut, width), dt)] * 2
             + [pltpu.SemaphoreType.DMA((30,))] * 2
         ),
         compiler_params=pltpu.CompilerParams(
-            collective_id=2, has_side_effects=True, vmem_limit_bytes=28 << 20
+            collective_id=2, has_side_effects=True, vmem_limit_bytes=20 << 20
         ),
-    )(part.reshape(2, 4, 2, slab, width), weight)
-
-
-CHUNK = 32
+    )(total, weight)
+
+
+STEP = 32
 
 
 def product_kernel(
-    transposed, unroll, source_ref, target_ref, count_ref, panel, tile_hbm, out,
-    tiles, total, tile_sem,
+    transposed, source_ref, target_ref, count_ref, panel, tiles, total
 ):
-    slots = tile_hbm.shape[0]
+    slots = tiles.shape[0]
     blocks = panel.shape[0]
-    chunks = slots // CHUNK
     live = count_ref[0, 0]
-
-    def tile_copy(c):
-        part = pl.ds(c * CHUNK, CHUNK)
-        return pltpu.make_async_copy(tile_hbm.at[part], tiles.at[part], tile_sem.at[c])
-
-    for c in range(chunks):
-        pl.when(c * CHUNK < live)(lambda c=c: tile_copy(c).start())
 
     @pl.loop(0, blocks)
     def _(g):
@@ -527,52 +550,35 @@
 
     dims = (((0,), (0,)), ((), ())) if transposed else (((1,), (0,)), ((), ()))
 
-    def some_slots(first):
-        products, targets = [], []
-        for k in range(unroll):
-            slot = first + k
-            products.append(lax.dot_general(
-                tiles[slot], panel[source_ref[0, slot]], dims, preferred_element_type=jnp.float32
-            ))
-            targets.append(jnp.where(slot < live, target_ref[0, slot], blocks))
-        for k in range(unroll):
-            total[targets[k]] += products[k]
-
-    def one_chunk(c):
-        tile_copy(c).wait()
-        if unroll == CHUNK:
-            some_slots(c * CHUNK)
-        else:
-            @pl.loop(0, CHUNK // unroll)
-            def _(step):
-                first = c * CHUNK + step * unroll
-                pl.when(first < live)(lambda: some_slots(first))
-
-    @pl.loop(0, chunks)
-    def _(c):
-        pl.when(c * CHUNK < live)(lambda: one_chunk(c))
-
-    @pl.loop(0, blocks)
-    def _(g):
-        out[g] = total[g].astype(out.dtype)
-
-
-def block_product(panel, tiles, source_ids, target_ids, count, transposed, unroll=32):
+    @pl.loop(0, slots // STEP)
+    def _(step):
+        first = step * STEP
+
+        @pl.when(first < live)
+        def _():
+            products, targets = [], []
+            for k in range(STEP):
+                slot = first + k
+                products.append(lax.dot_general(
+                    tiles[slot], panel[source_ref[0, slot]], dims,
+                    preferred_element_type=jnp.float32,
+                ))
+                targets.append(jnp.where(slot < live, target_ref[0, slot], blocks))
+            for k in range(STEP):
+                total[targets[k]] += products[k]
+
+
+def block_product(panel, tiles, source_ids, target_ids, count, transposed):
     slots, block, _ = tiles.shape
     blocks, _, width = panel.shape
     smem = pl.BlockSpec(memory_space=pltpu.SMEM)
     vmem = pl.BlockSpec(memory_space=pltpu.VMEM)
     return pl.pallas_call(
-        functools.partial(product_kernel, transposed, unroll),
-        out_shape=jax.ShapeDtypeStruct(panel.shape, panel.dtype),
-        in_specs=[smem, smem, smem, vmem, pl.BlockSpec(memory_space=pl.ANY)],
+        functools.partial(product_kernel, transposed),
+        out_shape=jax.ShapeDtypeStruct((blocks + 1, block, width), jnp.float32),
+        in_specs=[smem, smem, smem, vmem, vmem],
         out_specs=vmem,
-        scratch_shapes=[
-            pltpu.VMEM(tiles.shape, tiles.dtype),
-            pltpu.VMEM((blocks + 1, block, width), jnp.float32),
-            pltpu.SemaphoreType.DMA((slots // CHUNK,)),
-        ],
-        compiler_params=pltpu.CompilerParams(vmem_limit_bytes=36 << 20),
+        compiler_params=pltpu.CompilerParams(vmem_limit_bytes=26 << 20),
         cost_estimate=pl.CostEstimate(
             flops=2 * slots * block * block * width, transcendentals=0,
             bytes_accessed=2 * (tiles.size + 2 * panel.size),
@@ -590,11 +596,11 @@
     partial_one = block_product(
         row_panel.reshape(-1, block, width), tiles, rows, cols, block_counts, True
     )
-    col_panel = row_exchange(partial_one.reshape(-1, slab, width), weight_one)
+    col_panel = row_exchange(partial_one, weight_one, slab)
     partial_two = block_product(
         col_panel.reshape(-1, block, width), tiles, cols, rows, block_counts, False
     )
-    return col_sum(partial_two.reshape(-1, slab, width), weight_two)
+    return col_sum(partial_two, weight_two, slab)
 
 
 def solution(mesh):

time: 175 us -> 172 us (0.983)
  Pallas kernels: 170 us -> 168 us
where the time goes in v8:
time: 172 us; the launch traced here: 171 us
  Pallas kernels  168 us (98%)
  local copies, waits for them, and re-layouts  2.59 us (2%)
    pallas_call x1, Pallas kernels, row_exchange(): pl.pallas_call(row_kernel, out_shape=jax.ShapeDtypeStruct((2, 2, 4, slab,...  102 us
    pallas_call x1, Pallas kernels, col_sum(): pl.pallas_call(sum_kernel, out_shape=jax.ShapeDtypeStruct((slab, width),...  29.6 us
    pallas_call x1, Pallas kernels, col_gather(): pl.pallas_call(gather_kernel, out_shape=jax.ShapeDtypeStruct((2, 4, 2, sl...  28.6 us
    pallas_call x2, Pallas kernels, block_product(): pl.pallas_call(functools.partial(product_kernel, transposed), out_shape=j...  7.74 us

profile of v8, /device:TPU:1, one launch (start us, length us, event | category | flops | bytes accessed | tf_op | source)
XLA Modules:
  0.0 171.1 jit_solution(17183894885741429729)
XLA Ops:
  0.0 0.0 copy-start
  0.8 0.0 copy-start.1
  0.8 1.1 copy-done.1
  1.9 0.0 copy-start.6
  1.9 0.7 copy-done.6
  2.6 0.0 copy-start.4
  2.6 0.0 copy-start.5
  2.6 28.6 %shard_map.82 = bf16[2,4,2,768,256]{4,3,2,1,0:T(8,128)(2,1)S(1)} custom-call(s32[1,768]{1,0:T(1,128)S(1)} %copy-done.6, bf16[768,256]{1,0:T(8,128)(2,1)S(1)} %copy-done.1), custom_call_target="tpu_custom_call" | custom-call | tf_op jit(solution)/shard_map/pallas_call | solution.py:399
  31.3 0.0 copy-done
  31.3 0.0 copy-done.4
  31.3 0.0 copy-done.5
  31.3 0.0 copy-start.2
  31.3 3.8 %shard_map.83.total = f32[97,128,256]{2,1,0:T(8,128)S(1)} custom-call(s32[1,192]{1,0:T(1,128)S(1)} %bitcast.11, s32[1,192]{1,0:T(1,128)S(1)} %bitcast.9, s32[1,1]{1,0:T(1,128)S(6)} %copy.10.count_ref, bf16[96,128,256]{2,1,0:T(8,128)(2,1)S(1)} %bitcast.8, bf16[192,128,128]{2,1,0:T(8,128)(2,1)S(1)} %bitcast.5), custom_call_target="tpu_custom_call" | custom-call | flops 1610612736 | bytes 18874368 | tf_op jit(solution)/shard_map/pallas_call | solution.py:576
  35.1 0.0 copy-done.2
  35.1 101.7 %shard_map.84 = bf16[2,2,4,768,256]{4,3,2,1,0:T(8,128)(2,1)S(1)} custom-call(f32[97,128,256]{2,1,0:T(8,128)S(1)} %shard_map.83.total, bf16[256,256]{1,0:T(8,128)(2,1)S(1)} %copy-done.2), custom_call_target="tpu_custom_call" | custom-call | tf_op jit(solution)/shard_map/pallas_call | solution.py:272
  136.8 0.0 copy-start.3
  136.8 3.9 %shard_map.85.total = f32[97,128,256]{2,1,0:T(8,128)S(1)} custom-call(s32[1,192]{1,0:T(1,128)S(1)} %bitcast.10, s32[1,192]{1,0:T(1,128)S(1)} %bitcast.12, s32[1,1]{1,0:T(1,128)S(6)} %copy.10.count_ref, bf16[96,128,256]{2,1,0:T(8,128)(2,1)S(1)} %bitcast.7, bf16[192,128,128]{2,1,0:T(8,128)(2,1)S(1)} %bitcast.6), custom_call_target="tpu_custom_call" | custom-call | flops 1610612736 | bytes 18874368 | tf_op jit(solution)/shard_map/pallas_call | solution.py:576
  140.7 0.0 copy-done.3
  140.8 29.6 %shard_map.86 = bf16[768,256]{1,0:T(8,128)(2,1)S(1)} custom-call(f32[97,128,256]{2,1,0:T(8,128)S(1)} %shard_map.85.total, bf16[256,256]{1,0:T(8,128)(2,1)S(1)} %copy-done.3), custom_call_target="tpu_custom_call" | custom-call | tf_op jit(solution)/shard_map/pallas_call | solution.py:520
  170.3 0.7 copy.11
Async XLA Ops:
  0.0 31.3 %copy-start = (bf16[1,1,192,128,128]{4,3,2,1,0:T(8,128)(2,1)S(1)}, bf16[1,1,192,128,128]{4,3,2,1,0:T(8,128)(2,1)}, u32[]{:S(2)}) copy-start(bf16[1,1,192,128,128]{4,3,2,1,0:T(8,128)(2,1)} %param.13) | copy-start | bytes 18874372
  0.8 1.1 copy-start.1
  1.9 0.7 copy-start.6
  2.6 28.6 %copy-start.4 = (s32[1,1,192]{2,1,0:T(1,128)S(1)}, s32[1,1,192]{2,1,0:T(1,128)}, u32[]{:S(2)}) copy-start(s32[1,1,192]{2,1,0:T(1,128)} %param.11) | copy-start | bytes 2308
  2.6 28.6 %copy-start.5 = (s32[1,1,192]{2,1,0:T(1,128)S(1)}, s32[1,1,192]{2,1,0:T(1,128)}, u32[]{:S(2)}) copy-start(s32[1,1,192]{2,1,0:T(1,128)} %param.10) | copy-start | bytes 2308
  31.3 3.9 %copy-start.2 = (bf16[256,256]{1,0:T(8,128)(2,1)S(1)}, bf16[256,256]{1,0:T(8,128)(2,1)}, u32[]{:S(2)}) copy-start(bf16[256,256]{1,0:T(8,128)(2,1)} %weight.2) | copy-start | bytes 393220
  136.8 3.9 %copy-start.3 = (bf16[256,256]{1,0:T(8,128)(2,1)S(1)}, bf16[256,256]{1,0:T(8,128)(2,1)}, u32[]{:S(2)}) copy-start(bf16[256,256]{1,0:T(8,128)(2,1)} %weight.3) | copy-start | bytes 393220

commit v9 on v8

--- a/solution.py
+++ b/solution.py
@@ -9,19 +9,20 @@
 MESH = pl.DeviceIdType.MESH
 PARTS = 4
 ORDER = (
-    ("r1z", 0), ("r1o", 0), ("r1z", 2), ("r1z", 3), ("r1x", 0), ("r2", 0), ("r1o", 3), ("r1o", 2),
-    ("r2", 2), ("r3", 0), ("r1z", 1), ("r1x", 2), ("r3", 2), ("r4", 0), ("r2", 3), ("r1o", 1),
-    ("r1x", 3), ("r5", 0), ("r2", 1), ("r4", 2), ("r3", 3), ("d", 0), ("r5", 2), ("r1x", 1),
-    ("r3", 1), ("g2", 0), ("r4", 3), ("d", 2), ("g3o", 0), ("r5", 3), ("g2", 2), ("g4", 2),
-    ("r4", 1), ("g4", 0), ("g4o", 0), ("g3", 0), ("d", 3), ("g3o", 2), ("r5", 1), ("g2", 3),
-    ("g3", 2), ("g4", 3), ("g5", 2), ("d", 1), ("g3o", 3), ("g5", 3), ("g3", 3), ("g2", 1),
-    ("g4", 1), ("g5", 0), ("g3", 1), ("g4o", 2), ("g3o", 1), ("g5", 1), ("g4o", 3), ("g4o", 1),
+    ("r1o", 0), ("r1z", 0), ("r1x", 0), ("r1o", 2), ("r1z", 2), ("r2", 0), ("r1o", 1), ("r1o", 3),
+    ("r1z", 1), ("r2", 2), ("r1z", 3), ("r3", 0), ("r1x", 2), ("r3", 2), ("r2", 1), ("r4", 0),
+    ("r2", 3), ("r1x", 3), ("r5", 0), ("r4", 2), ("r3", 3), ("r1x", 1), ("d", 0), ("r5", 2),
+    ("r3", 1), ("r4", 3), ("g3", 0), ("g2", 0), ("dx", 0), ("r5", 3), ("r4", 1), ("g3o", 0),
+    ("d", 2), ("dx", 2), ("g4", 2), ("r5", 1), ("g4", 0), ("d", 3), ("dx", 3), ("g3", 2), ("g2", 2),
+    ("d", 1), ("g3p", 0), ("g4", 3), ("g3", 3), ("g3o", 2), ("g2", 3), ("g2", 1), ("dx", 1),
+    ("g3", 1), ("g5", 2), ("g5", 0), ("g4", 1), ("g3o", 3), ("g3o", 1), ("g4o", 2), ("g5", 3),
+    ("g3p", 2), ("g5", 1), ("g4o", 0), ("g3p", 3), ("g3p", 1), ("g4o", 3), ("g4o", 1),
 )
 
 
 class Mail:
     def __init__(self, send_sem, recv_sem):
-        self.send_sem, self.recv_sem, self.sent = send_sem, recv_sem, {}
+        self.send_sem, self.recv_sem, self.sent, self.arrived = send_sem, recv_sem, {}, set()
 
     def send(self, name, src, dst, device):
         slot = len(self.sent)
@@ -34,7 +35,9 @@
 
     def await_recv(self, *names):
         for name in names:
-            self.sent[name].wait_recv()
+            if name not in self.arrived:
+                self.sent[name].wait_recv()
+                self.arrived.add(name)
 
     def finish(self):
         for copy in self.sent.values():
@@ -178,16 +181,19 @@
         mail.await_recv(("r5ar", p), ("r5al", p))
         dense_relu(hid.at[a], (mine.at[pl.ds(0, h)], r5a_l.at[p], r5a_r.at[p]), weight)
         mail.send(("g1ar", p), hid.at[a], at(out, z, x, a), to_zr)
-        mail.send(("g3ar", p), hid.at[a], at(out, z, x, a), to_xr)
         mail.await_recv(("r5br", p), ("r5bl", p))
         dense_relu(hid.at[b], (mine.at[pl.ds(h, h)], r5b_l.at[p], r5b_r.at[p]), weight)
         mail.send(("g1bl", p), hid.at[b], at(out, z, x, b), to_zl)
-        mail.send(("g3bl", p), hid.at[b], at(out, z, x, b), to_xl)
         mail.send(("g1br", p), hid.at[b], at(out, z, x, b), to_zr)
         mail.send(("g1al", p), hid.at[a], at(out, z, x, a), to_zl)
+        pltpu.make_async_copy(hid.at[n_], at(out, z, x, n_), hid_sem.at[p]).start()
+
+    def dense_x(p):
+        n_, a, b = rows(p)
+        mail.send(("g3ar", p), hid.at[a], at(out, z, x, a), to_xr)
+        mail.send(("g3bl", p), hid.at[b], at(out, z, x, b), to_xl)
         mail.send(("g3br", p), hid.at[b], at(out, z, x, b), to_xr)
         mail.send(("g3al", p), hid.at[a], at(out, z, x, a), to_xl)
-        pltpu.make_async_copy(hid.at[n_], at(out, z, x, n_), hid_sem.at[p]).start()
 
     def pass_on(name, p, zs, xs, rows_, to):
         mail.send((name, p), at(out, zs, xs, rows_), at(out, zs, xs, rows_), to)
@@ -214,7 +220,7 @@
 
     def g3(p):
         n_, a, b = rows(p)
-        mail.await_recv(("g1br", p), ("g1al", p))
+        mail.await_recv(("g1ar", p), ("g1bl", p), ("g1br", p), ("g1al", p))
         both = out.at[:, other, x, n_]
         mail.send(("g3mr", p), both, both, to_xr)
         mail.send(("g3ml", p), both, both, to_xl)
@@ -225,6 +231,9 @@
         pass_on("g3oar", p, zo, x, a, to_xr)
         mail.await_recv(("g2l", p))
         pass_on("g3obl", p, zo, x, b, to_xl)
+
+    def g3p(p):
+        n_, a, b = rows(p)
         pass_on("g3obr", p, zo, x, b, to_xr)
         pass_on("g3oal", p, zo, x, a, to_xl)
 
@@ -243,8 +252,8 @@
         )))
 
     stages = dict(
-        r1z=r1z, r1o=r1o, r1x=r1x, r2=r2, r3=r3, r4=r4, r5=r5, d=dense, g2=g2, g4=g4, g5=g5, g3=g3,
-        g3o=g3o, g4o=g4o,
+        r1z=r1z, r1o=r1o, r1x=r1x, r2=r2, r3=r3, r4=r4, r5=r5, d=dense, dx=dense_x, g2=g2, g4=g4, g5=g5,
+        g3=g3, g3o=g3o, g3p=g3p, g4o=g4o,
     )
     first_x = next(i for i, (name, _) in enumerate(ORDER) if name == "r1x")
     for i, (name, p) in enumerate(ORDER):
@@ -534,7 +543,7 @@
     )(total, weight)
 
 
-STEP = 32
+STEP = 64
 
 
 def product_kernel(

time: 172 us -> 171 us (level)
  no operation moved by 1% of the time
where the time goes in v9:
time: 171 us
  Pallas kernels  168 us (98%)
  local copies, waits for them, and re-layouts  2.59 us (2%)
    pallas_call x1, Pallas kernels, row_exchange(): pl.pallas_call(row_kernel, out_shape=jax.ShapeDtypeStruct((2, 2, 4, slab,...  100 us
    pallas_call x1, Pallas kernels, col_sum(): pl.pallas_call(sum_kernel, out_shape=jax.ShapeDtypeStruct((slab, width),...  30.3 us
    pallas_call x1, Pallas kernels, col_gather(): pl.pallas_call(gather_kernel, out_shape=jax.ShapeDtypeStruct((2, 4, 2, sl...  28.6 us
    pallas_call x2, Pallas kernels, block_product(): pl.pallas_call(functools.partial(product_kernel, transposed), out_shape=j...  8.5 us

profile of v9, /device:TPU:1, one launch (start us, length us, event | category | flops | bytes accessed | tf_op | source)
XLA Modules:
  0.0 171.3 jit_solution(10280478667578101980)
XLA Ops:
  0.0 0.0 copy-start
  0.8 0.0 copy-start.1
  0.8 1.1 copy-done.1
  1.9 0.0 copy-start.6
  1.9 0.7 copy-done.6
  2.6 0.0 copy-start.4
  2.6 0.0 copy-start.5
  2.6 28.6 %shard_map.82 = bf16[2,4,2,768,256]{4,3,2,1,0:T(8,128)(2,1)S(1)} custom-call(s32[1,768]{1,0:T(1,128)S(1)} %copy-done.6, bf16[768,256]{1,0:T(8,128)(2,1)S(1)} %copy-done.1), custom_call_target="tpu_custom_call" | custom-call | tf_op jit(solution)/shard_map/pallas_call | solution.py:408
  31.3 0.0 copy-done
  31.3 0.0 copy-done.4
  31.3 0.0 copy-done.5
  31.3 0.0 copy-start.2
  31.3 4.1 %shard_map.83.total = f32[97,128,256]{2,1,0:T(8,128)S(1)} custom-call(s32[1,192]{1,0:T(1,128)S(1)} %bitcast.11, s32[1,192]{1,0:T(1,128)S(1)} %bitcast.9, s32[1,1]{1,0:T(1,128)S(6)} %copy.10.count_ref, bf16[96,128,256]{2,1,0:T(8,128)(2,1)S(1)} %bitcast.8, bf16[192,128,128]{2,1,0:T(8,128)(2,1)S(1)} %bitcast.5), custom_call_target="tpu_custom_call" | custom-call | flops 1610612736 | bytes 18874368 | tf_op jit(solution)/shard_map/pallas_call | solution.py:585
  35.4 0.0 copy-done.2
  35.5 100.4 %shard_map.84 = bf16[2,2,4,768,256]{4,3,2,1,0:T(8,128)(2,1)S(1)} custom-call(f32[97,128,256]{2,1,0:T(8,128)S(1)} %shard_map.83.total, bf16[256,256]{1,0:T(8,128)(2,1)S(1)} %copy-done.2), custom_call_target="tpu_custom_call" | custom-call | tf_op jit(solution)/shard_map/pallas_call | solution.py:281
  135.8 0.0 copy-start.3
  135.9 4.4 %shard_map.85.total = f32[97,128,256]{2,1,0:T(8,128)S(1)} custom-call(s32[1,192]{1,0:T(1,128)S(1)} %bitcast.10, s32[1,192]{1,0:T(1,128)S(1)} %bitcast.12, s32[1,1]{1,0:T(1,128)S(6)} %copy.10.count_ref, bf16[96,128,256]{2,1,0:T(8,128)(2,1)S(1)} %bitcast.7, bf16[192,128,128]{2,1,0:T(8,128)(2,1)S(1)} %bitcast.6), custom_call_target="tpu_custom_call" | custom-call | flops 1610612736 | bytes 18874368 | tf_op jit(solution)/shard_map/pallas_call | solution.py:585
  140.2 0.0 copy-done.3
  140.2 30.3 %shard_map.86 = bf16[768,256]{1,0:T(8,128)(2,1)S(1)} custom-call(f32[97,128,256]{2,1,0:T(8,128)S(1)} %shard_map.85.total, bf16[256,256]{1,0:T(8,128)(2,1)S(1)} %copy-done.3), custom_call_target="tpu_custom_call" | custom-call | tf_op jit(solution)/shard_map/pallas_call | solution.py:529
  170.5 0.7 copy.11
Async XLA Ops:
  0.0 31.3 %copy-start = (bf16[1,1,192,128,128]{4,3,2,1,0:T(8,128)(2,1)S(1)}, bf16[1,1,192,128,128]{4,3,2,1,0:T(8,128)(2,1)}, u32[]{:S(2)}) copy-start(bf16[1,1,192,128,128]{4,3,2,1,0:T(8,128)(2,1)} %param.13) | copy-start | bytes 18874372
  0.8 1.1 copy-start.1
  1.9 0.7 copy-start.6
  2.6 28.6 %copy-start.4 = (s32[1,1,192]{2,1,0:T(1,128)S(1)}, s32[1,1,192]{2,1,0:T(1,128)}, u32[]{:S(2)}) copy-start(s32[1,1,192]{2,1,0:T(1,128)} %param.11) | copy-start | bytes 2308
  2.6 28.6 %copy-start.5 = (s32[1,1,192]{2,1,0:T(1,128)S(1)}, s32[1,1,192]{2,1,0:T(1,128)}, u32[]{:S(2)}) copy-start(s32[1,1,192]{2,1,0:T(1,128)} %param.10) | copy-start | bytes 2308
  31.3 4.2 %copy-start.2 = (bf16[256,256]{1,0:T(8,128)(2,1)S(1)}, bf16[256,256]{1,0:T(8,128)(2,1)}, u32[]{:S(2)}) copy-start(bf16[256,256]{1,0:T(8,128)(2,1)} %weight.2) | copy-start | bytes 393220
  135.8 4.4 %copy-start.3 = (bf16[256,256]{1,0:T(8,128)(2,1)S(1)}, bf16[256,256]{1,0:T(8,128)(2,1)}, u32[]{:S(2)}) copy-start(bf16[256,256]{1,0:T(8,128)(2,1)} %weight.3) | copy-start | bytes 393220
